TPU v7x, 768 devices: a whole 4x8x12 slice. The times are simulated.
768 devices in a mesh: shard: 16 (over y, core), rep: 48 (over z, x).
Axes of the slice: x: 4, y: 8, z: 12, core: 2. Of those that a mesh axis runs over, the one named last changes fastest.
Arguments:
- node_feats: bfloat16 [196608, 512], P(('shard', 'rep')), may hold values from -6 to 6
- send_rows: int32 [768, 16, 32], P(('shard', 'rep')), may hold values from 0 to 255
- neighbors: int32 [196608, 16], P(('shard', 'rep')), may hold values from 0 to 767
- neighbor_weight: float32 [196608, 16], P(('shard', 'rep')), may hold values from 0.1 to 1
- gcn_weight: bfloat16 [1024, 512], replicated, may hold values from -0.1875 to 0.1875
- user_dense: bfloat16 [6144, 512], P(('shard', 'rep')), may hold values from -6 to 6
- cand_owner: int32 [6144, 50, 1], P(('shard', 'rep')), may hold values from 0 to 15; in each aligned block of 400 rows (0 to 399, 400 to 799, ..., all dimensions but the last counted through in order) at most 56 rows name the same one
- cand_row: int32 [6144, 50], P(('shard', 'rep')), may hold values from 0 to 255
- mlp_weight: bfloat16 [1787, 1024], replicated, may hold values from -0.125 to 0.125
- out_weight: bfloat16 [1024], replicated, may hold values from -0.1875 to 0.1875
- logit_grad: float32 [6144], P(('shard', 'rep')), may hold values from -384 to 384
Outputs:
- item_embedding: bfloat16 [196608, 512], P(('shard', 'rep'))
- embedding_grad: float32 [196608, 512], P(('shard', 'rep'))
- click_logits: float32 [6144], P(('shard', 'rep'))
- gcn_weight_grad: float32 [1024, 512], replicated
Inputs may be any that keep to these rules, and one draw needn't show every extreme that they name: `cand_owner`: among the candidates of one device's 8 requests, no owner is named more than 56 times, a bound that some block reaches.
All inputs are finite; a program needn't handle non-finite values.
Results may differ from a plain program's by a relative error of at most 0.015.
Values may be sent and summed in bfloat16 or wider, within the bound.
A program may use at most 32 MiB of HBM per device.

v0:
```python
import math

import jax
import jax.numpy as jnp
import numpy as np
from jax import lax
from jax.sharding import PartitionSpec as P


def pair_tables(count):
    lower_i, lower_j = np.tril_indices(count, -1)
    pair_table = (lower_i * count + lower_j).astype(np.int32)
    sym_table = np.full((count * count,), lower_i.shape[0], dtype=np.int32)
    sym_table[lower_i * count + lower_j] = np.arange(lower_i.shape[0])
    sym_table[lower_j * count + lower_i] = np.arange(lower_i.shape[0])
    return (pair_table, sym_table)


def normalize(projected):
    return projected * lax.rsqrt(jnp.mean(projected * projected, axis=-1, keepdims=True) + 1e-06)


def local_layer(tables, own_rows, indices, weights, gcn_weight):
    picked = tables[indices].astype(jnp.float32)
    summed = jnp.sum(weights[:, :, None] * picked, axis=1)
    aggregated = (summed / jnp.sum(weights, axis=1)[:, None]).astype(jnp.bfloat16)
    joined = jnp.concatenate([own_rows, aggregated], axis=1)
    projected = jnp.dot(joined, gcn_weight, preferred_element_type=jnp.float32)
    return (joined, projected)


def on_device(
    node_feats,
    send_rows,
    neighbors,
    neighbor_weight,
    gcn_weight,
    user_dense,
    cand_owner,
    cand_row,
    mlp_weight,
    out_weight,
    logit_grad,
):
    peer_count = lax.axis_size("shard")
    node_count, model_width = node_feats.shape
    outgoing = node_feats[send_rows[0].reshape(-1)].reshape(peer_count, -1, model_width)
    incoming = lax.all_to_all(outgoing, "shard", split_axis=0, concat_axis=0, tiled=True)
    tables = jnp.concatenate([node_feats, incoming.reshape(-1, model_width)], axis=0)
    joined, projected = local_layer(tables, node_feats, neighbors, neighbor_weight, gcn_weight)
    embeddings = normalize(projected).astype(jnp.bfloat16)
    requests, candidates = cand_row.shape
    capacity = 9 * requests * candidates // (4 * peer_count)
    owners = cand_owner.reshape(-1)
    wanted_rows = cand_row.reshape(-1)
    owner_hits = (owners[:, None] == jnp.arange(peer_count, dtype=jnp.int32)[None, :]).astype(
        jnp.int32
    )
    slot_rank = jnp.sum(jnp.cumsum(owner_hits, axis=0) * owner_hits, axis=1) - 1
    slot_of = owners * capacity + slot_rank
    wanted = (
        jnp.zeros((peer_count * capacity,), jnp.int32)
        .at[slot_of]
        .set(wanted_rows)
        .reshape(peer_count, capacity)
    )
    asked = lax.all_to_all(wanted, "shard", split_axis=0, concat_axis=0, tiled=True)
    looked_up = embeddings[asked]
    returned = lax.all_to_all(looked_up, "shard", split_axis=0, concat_axis=0, tiled=True)
    cand_rows = returned.reshape(peer_count * capacity, model_width)[slot_of].reshape(
        requests, candidates, model_width
    )
    stacked = jnp.concatenate([user_dense[:, None, :], cand_rows], axis=1)
    scale = math.sqrt(model_width)
    grams = jnp.einsum("qid,qjd->qij", stacked, stacked, preferred_element_type=jnp.float32) / scale
    pair_table, sym_table = pair_tables(candidates + 1)
    lower_part = grams.reshape(requests, -1)[:, pair_table]
    mixed = jnp.concatenate([user_dense, lower_part.astype(jnp.bfloat16)], axis=1)
    hidden_pre = jnp.dot(mixed, mlp_weight, preferred_element_type=jnp.float32)
    hidden_act, gelu_back = jax.vjp(jax.nn.gelu, hidden_pre)
    hidden = hidden_act.astype(jnp.bfloat16)
    click_logits = jnp.dot(hidden, out_weight, preferred_element_type=jnp.float32)
    hidden_grad = gelu_back(logit_grad[:, None] * out_weight.astype(jnp.float32)[None, :])[
        0
    ].astype(jnp.bfloat16)
    mixed_grad = lax.dot_general(
        hidden_grad, mlp_weight, (((1,), (1,)), ((), ())), preferred_element_type=jnp.float32
    )
    lower_grad = jnp.concatenate(
        [mixed_grad[:, model_width:], jnp.zeros((requests, 1), jnp.float32)], axis=1
    )
    sym_grad = (
        lower_grad[:, sym_table]
        .reshape(requests, candidates + 1, candidates + 1)
        .astype(jnp.bfloat16)
    )
    stacked_grad = (
        jnp.einsum("qij,qjd->qid", sym_grad, stacked, preferred_element_type=jnp.float32) / scale
    )
    cand_grad = stacked_grad[:, 1:].astype(jnp.bfloat16).reshape(-1, model_width)
    outboxes = (
        jnp.zeros((peer_count * capacity, model_width), jnp.bfloat16).at[slot_of].set(cand_grad)
    )
    inboxes = lax.all_to_all(
        outboxes.reshape(peer_count, capacity, model_width),
        "shard",
        split_axis=0,
        concat_axis=0,
        tiled=True,
    )
    embed_grad = (
        jnp.zeros((node_count, model_width), jnp.float32)
        .at[asked.reshape(-1)]
        .add(inboxes.reshape(-1, model_width).astype(jnp.float32))
    )
    unused, norm_back = jax.vjp(normalize, projected)
    pre_norm_grad = norm_back(embed_grad)[0].astype(jnp.bfloat16)
    grad_term = lax.dot_general(
        joined, pre_norm_grad, (((0,), (0,)), ((), ())), preferred_element_type=jnp.float32
    )
    summed_grad = lax.psum(grad_term, ("shard", "rep"))
    gcn_weight_grad = summed_grad / (peer_count * lax.axis_size("rep"))
    return (embeddings, embed_grad, click_logits, gcn_weight_grad)


def solution(mesh):
    return jax.shard_map(
        on_device,
        mesh=mesh,
        in_specs=(
            P(("shard", "rep"), None),
            P(("shard", "rep"), None, None),
            P(("shard", "rep"), None),
            P(("shard", "rep"), None),
            P(),
            P(("shard", "rep"), None),
            P(("shard", "rep"), None, None),
            P(("shard", "rep"), None),
            P(),
            P(),
            P(("shard", "rep")),
        ),
        out_specs=(P(("shard", "rep"), None), P(("shard", "rep"), None), P(("shard", "rep")), P()),
        check_vma=False,
    )
```

profile of v0, /device:TPU:1, one launch (start us, length us, event | category | flops | bytes accessed | tf_op | source)
XLA Modules:
  0.0 660.8 jit_solution(12767186215116230667)
XLA Ops:
  7.2 0.0 copy-start
  7.2 0.5 broadcast.238
  7.7 1.4 fusion.59
  9.1 0.1 eq.22
  9.2 1.2 reduce-window.6
  10.3 0.2 slice_reduce_fusion
  10.6 0.1 bitcast_bitcast_fusion
  10.7 0.1 mul.131
  10.8 0.8 reshape.260
  11.6 2.9 scatter_custom_fusion
  14.5 0.7 all_to_all.18
  15.2 13.8 %all-to-all-start.1 = ((s32[16,1,56]{2,1,0:T(1,128)}), s32[16,1,56]{2,1,0:T(1,128)S(1)}, u32[]{:S(2)}, u32[]{:S(2)}) async-start(s32[16,1,56]{2,1,0:T(1,128)} %all_to_all.18), calls=%async_computation.1 | async-start | bytes 16384 | tf_op jit(solution)/shard_map/all_to_all | solution.py:67
  29.0 0.8 reshape_squeeze.3
  29.8 0.0 copy-start.5
  29.8 2.6 gather_fusion
  32.4 3.5 all-to-all-done.1
  35.9 4.0 all-to-all-start
  40.0 0.1 copy.34
  40.1 0.1 reshape.218
  40.2 0.1 copy.33
  40.3 0.1 reshape.226
  40.4 16.9 %all-to-all-done = bf16[16,32,512]{2,1,0:T(8,128)(2,1)S(1)} async-done(((bf16[16,32,512]{2,1,0:T(8,128)(2,1)}), bf16[16,32,512]{2,1,0:T(8,128)(2,1)S(1)}, u32[]{:S(2)}, u32[]{:S(2)}) %all-to-all-start) | async-done | bytes 524320 | tf_op jit(solution)/shard_map/all_to_all | solution.py:48
  57.3 0.1 pad_maximum_fusion
  57.4 17.3 %gather_fusion.1 = bf16[4096,512]{1,0:T(8,128)(2,1)} fusion(bf16[768,512]{1,0:T(8,128)(2,1)S(1)} %pad_maximum_fusion, s32[4096]{0:T(1024)S(1)} %broadcast_clamp_fusion), kind=kCustom, calls=%fused_computation.1 | custom fusion | bytes 8404992 | tf_op jit(solution)/shard_map/gather | solution.py:24
  74.6 3.5 fusion
  78.1 0.1 divide_convert_fusion
  78.2 0.5 multiply_reduce_fusion.1
  78.8 0.1 multiply_convert_fusion
  78.9 0.0 copy-start.12
  78.9 0.0 copy-start.10
  79.0 4.0 gather_fusion.2
  82.9 3.7 all-to-all-start.2
  86.8 24.4 %all-to-all-done.2 = bf16[16,56,512]{2,1,0:T(8,128)(2,1)S(1)} async-done(((bf16[16,56,512]{2,1,0:T(8,128)(2,1)}), bf16[16,56,512]{2,1,0:T(8,128)(2,1)S(1)}, u32[]{:S(2)}, u32[]{:S(2)}) %all-to-all-start.2) | async-done | bytes 917536 | tf_op jit(solution)/shard_map/all_to_all | solution.py:69
  111.2 2.1 gather_fusion.3
  113.2 0.1 reshape.202
  113.4 0.3 convolution_multiply_fusion
  113.7 0.2 reshape.203
  113.8 0.4 copy.38
  114.2 3.5 gather_fusion.4
  117.8 1.1 copy.39
  118.9 2.8 fusion.27
  121.7 0.4 copy-done.4
  122.0 0.9 fusion.1
  122.9 0.1 concatenate.19.clone
  123.0 6.6 gather_fusion.5
  129.6 1.3 copy.41
  130.9 0.2 convert_element_type.46
  131.1 0.3 fusion.11
  131.4 0.1 fusion.5
  131.5 0.1 reshape.268
  131.7 3.0 scatter_custom_fusion.1
  134.7 3.5 all-to-all-start.3
  138.2 0.0 all-reduce.4.cloned.1.call-start
  138.3 0.7 reduce.15
  139.0 0.1 reshape.200
  139.1 24.3 %all-to-all-done.3 = bf16[16,56,512]{2,1,0:T(8,128)(2,1)S(1)} async-done(((bf16[16,56,512]{2,1,0:T(8,128)(2,1)}), bf16[16,56,512]{2,1,0:T(8,128)(2,1)S(1)}, u32[]{:S(2)}, u32[]{:S(2)}) %all-to-all-start.3) | async-done | bytes 917536 | tf_op jit(solution)/shard_map/all_to_all | solution.py:104
  163.3 7.3 %scatter_custom_fusion.2 = f32[256,512]{1,0:T(8,128)S(1)} fusion(s32[896]{0:T(1024)S(1)} %fusion.40, bf16[896,512]{1,0:T(8,128)(2,1)S(1)} %bitcast.44, f32[]{:T(128)} %constant.28.clone.1), kind=kCustom, calls=%fused_computation.13 | custom fusion | flops 917504 | bytes 1441796 | tf_op jit(solution)/shard_map/scatter-add | solution.py:114
  170.6 0.1 multiply_reduce_fusion
  170.7 0.7 multiply_multiply_fusion.4
  171.5 1.9 fusion.9
  173.3 0.0 all-reduce.4.cloned.1.call-update
  173.4 0.6 convolution_bitcast_fusion
  174.0 476.7 %all-reduce.4.cloned.1.call-done = f32[1024,512]{1,0:T(8,128)} async-done(((f32[1024,512]{1,0:T(8,128)}), f32[1024,512]{1,0:T(8,128)}) %all-reduce.4.cloned.1.call-update) | async-done | bytes 2097168 | tf_op jit(solution)/shard_map/psum | solution.py:121
  650.8 3.2 broadcast_multiply_fusion
  (47 shorter events, 0.3 us)
Async XLA Ops:
  7.2 71.1 %copy-start = (bf16[1024,512]{1,0:T(8,128)(2,1)S(1)}, bf16[1024,512]{1,0:T(8,128)(2,1)}, u32[]{:S(2)}) copy-start(bf16[1024,512]{1,0:T(8,128)(2,1)} %param.19) | copy-start | bytes 3145732
  7.2 22.6 %copy-start.2 = (bf16[256,512]{1,0:T(8,128)(2,1)S(1)}, bf16[256,512]{1,0:T(8,128)(2,1)}, u32[]{:S(2)}) copy-start(bf16[256,512]{1,0:T(8,128)(2,1)} %param.15) | copy-start | bytes 786436
  15.2 20.8 %all-to-all-start.1 = ((s32[16,1,56]{2,1,0:T(1,128)}), s32[16,1,56]{2,1,0:T(1,128)S(1)}, u32[]{:S(2)}, u32[]{:S(2)}) async-start(s32[16,1,56]{2,1,0:T(1,128)} %all_to_all.18), calls=%async_computation.1 | async-start | bytes 16384 | tf_op jit(solution)/shard_map/all_to_all | solution.py:67
  29.8 10.2 %copy-start.9 = (s32[256,16]{0,1:T(8,128)S(1)}, s32[256,16]{0,1:T(8,128)}, u32[]{:S(2)}) copy-start(s32[256,16]{0,1:T(8,128)} %param.17) | copy-start | bytes 49156
  29.8 10.4 %copy-start.5 = (f32[256,16]{0,1:T(8,128)S(1)}, f32[256,16]{0,1:T(8,128)}, u32[]{:S(2)}) copy-start(f32[256,16]{0,1:T(8,128)} %param.18) | copy-start | bytes 49156
  35.9 21.4 %all-to-all-start = ((bf16[16,32,512]{2,1,0:T(8,128)(2,1)}), bf16[16,32,512]{2,1,0:T(8,128)(2,1)S(1)}, u32[]{:S(2)}, u32[]{:S(2)}) async-start(bf16[16,32,512]{2,1,0:T(8,128)(2,1)} %bitcast.1), calls=%async_computation | async-start | bytes 1048576 | tf_op jit(solution)/shard_map/all_to_all | solution.py:48
  78.8 4.2 copy-start.13
  78.9 4.0 copy-start.1
  78.9 7.8 %copy-start.8 = (bf16[8,512]{1,0:T(8,128)(2,1)S(1)}, bf16[8,512]{1,0:T(8,128)(2,1)}, u32[]{:S(2)}) copy-start(bf16[8,512]{1,0:T(8,128)(2,1)} %param.20) | copy-start | bytes 24580
  78.9 7.8 %copy-start.11 = (bf16[1024]{0:T(1024)(128)(2,1)S(1)}, bf16[1024]{0:T(1024)(128)(2,1)}, u32[]{:S(2)}) copy-start(bf16[1024]{0:T(1024)(128)(2,1)} %param.24) | copy-start | bytes 6148
  78.9 7.8 %copy-start.12 = (s32[1275]{0:T(1024)S(1)}, s32[1275]{0:T(1024)}, u32[]{:S(2)}) copy-start(s32[1275]{0:T(1024)} %constant.89) | copy-start | bytes 15304
  78.9 7.8 %copy-start.10 = (s32[2601]{0:T(1024)S(1)}, s32[2601]{0:T(1024)}, u32[]{:S(2)}) copy-start(s32[2601]{0:T(1024)} %constant.90) | copy-start | bytes 31216
  82.9 28.2 %all-to-all-start.2 = ((bf16[16,56,512]{2,1,0:T(8,128)(2,1)}), bf16[16,56,512]{2,1,0:T(8,128)(2,1)S(1)}, u32[]{:S(2)}, u32[]{:S(2)}) async-start(bf16[16,56,512]{2,1,0:T(8,128)(2,1)} %bitcast.43), calls=%async_computation.2 | async-start | bytes 1835008 | tf_op jit(solution)/shard_map/all_to_all | solution.py:69
  113.7 8.0 %copy-start.14 = (f32[8]{0:T(128)S(1)}, f32[8]{0:T(128)}, u32[]{:S(2)}) copy-start(f32[8]{0:T(128)} %param.25) | copy-start | bytes 100
  118.9 3.2 copy-start.4
  122.0 7.5 %copy-start.6 = (f32[8,1024]{1,0:T(8,128)}, f32[8,1024]{1,0:T(8,128)S(1)}, u32[]{:S(2)}) copy-start(f32[8,1024]{1,0:T(8,128)S(1)} %fusion.27) | copy-start | bytes 98308
  134.7 28.7 %all-to-all-start.3 = ((bf16[16,56,512]{2,1,0:T(8,128)(2,1)}), bf16[16,56,512]{2,1,0:T(8,128)(2,1)S(1)}, u32[]{:S(2)}, u32[]{:S(2)}) async-start(bf16[16,56,512]{2,1,0:T(8,128)(2,1)} %bitcast.13), calls=%async_computation.3 | async-start | bytes 1835008 | tf_op jit(solution)/shard_map/all_to_all | solution.py:104
  138.2 512.6 %all-reduce.4.cloned.1.call-start = ((), (), s32[]{:S(2)}) async-start(), calls=%async_computation.4 | async-start | bytes 4194304 | tf_op jit(solution)/shard_map/psum | solution.py:121
  170.6 2.8 copy-start.3
  171.4 1.9 copy-start.7
Sparse Core Ops, SparseCore 0:
  173.5 477.2 all-reduce.3
where the time goes:
time: 663 us; the launch traced here: 661 us
  waiting for transfers between devices  546 us (82%)
  local copies, waits for them, and re-layouts  49.5 us (7%)
  starting transfers between devices  25.1 us (4%)
  other arithmetic  18.5 us (3%)
  between operations  14.5 us (2%)
  matrix products  7.36 us (1%)
    psum x1, waiting for transfers between devices, on_device(): summed_grad = lax.psum(grad_term, ('shard', 'rep'))  477 us
    all_to_all x1, waiting for transfers between devices, on_device(): lax.all_to_all(looked_up, 'shard', split_axis=0, concat_axis=0, tiled=True)  24.4 us
    all_to_all x1, waiting for transfers between devices, on_device(): lax.all_to_all(outboxes.reshape(peer_count, capacity, model_width), 'shar...  24.3 us
    gather x1, local copies, waits for them, and re-layouts, local_layer(): picked = tables[indices].astype(jnp.float32)  17.3 us
    all_to_all x1, waiting for transfers between devices, on_device(): lax.all_to_all(outgoing, 'shard', split_axis=0, concat_axis=0, tiled=True)  16.9 us
    all_to_all x1, starting transfers between devices, on_device(): lax.all_to_all(wanted, 'shard', split_axis=0, concat_axis=0, tiled=True)  13.8 us
  transfers between devices with their start and end apart: 5, of which 5 were waited for; matrix products, arithmetic and copies ran while one was open for 1% of the time, Pallas kernels for 0%

commit v1 on v0

--- a/solution.py
+++ b/solution.py
@@ -4,7 +4,163 @@
 import jax.numpy as jnp
 import numpy as np
 from jax import lax
+from jax.experimental import pallas as pl
+from jax.experimental.pallas import tpu as pltpu
 from jax.sharding import PartitionSpec as P
+
+
+CHUNKS = 2
+N_CORE, N_X, N_Y, N_Z = 2, 4, 8, 12
+MESH = pl.DeviceIdType.MESH
+
+
+def places():
+    shard, rep = lax.axis_index("shard"), lax.axis_index("rep")
+    return lax.div(shard, 2), lax.rem(shard, 2), lax.div(rep, 4), lax.rem(rep, 4)
+
+
+def reduce_kernel(
+    part_ref, out_ref, send0, recv0, half, send1, recv1, send2, recv2, slots3, fin4, fin5, fin6, s_sem, r_sem
+):
+    y, core, z, x = places()
+    other_core = {"shard": y * 2 + 1 - core}
+
+    def at_x(k):
+        return {"rep": z * 4 + lax.rem(x + k, N_X)}
+
+    def at_y(k):
+        return {"shard": lax.rem(y + k, N_Y) * 2 + core}
+
+    def at_z(k):
+        return {"rep": lax.rem(z + k, N_Z) * 4 + x}
+
+    peers = [other_core] + [at_x(k) for k in range(1, N_X)]
+    peers += [at_y(k) for k in range(1, N_Y)] + [at_z(k) for k in range(1, N_Z)]
+    barrier = pltpu.get_barrier_semaphore()
+    for peer in peers:
+        pl.semaphore_signal(barrier, inc=1, device_id=peer, device_id_type=MESH)
+    pl.semaphore_wait(barrier, len(peers))
+
+    rows, width = part_ref.shape
+    chunk = width // CHUNKS
+    wide = jnp.float32
+    thin = jnp.bfloat16
+    in_flight = {}
+
+    def send(c, number, src, dst, peer):
+        copy = pltpu.make_async_remote_copy(
+            src_ref=src,
+            dst_ref=dst,
+            send_sem=s_sem.at[c, number],
+            recv_sem=r_sem.at[c, number],
+            device_id=peer,
+            device_id_type=MESH,
+        )
+        copy.start()
+        in_flight[c, number] = copy
+
+    def arrive(c, numbers):
+        for number in numbers:
+            in_flight[c, number].wait()
+
+    def step0(c):
+        cols = pl.ds(c * chunk, chunk)
+        theirs = pl.multiple_of((1 - core) * (rows // 2), rows // 2)
+        send0[c] = part_ref[pl.ds(theirs, rows // 2), cols].astype(thin)
+        send(c, 0, send0.at[c], recv0.at[c], other_core)
+
+    def step1(c):
+        arrive(c, [0])
+        cols = pl.ds(c * chunk, chunk)
+        mine = pl.multiple_of(core * (rows // 2), rows // 2)
+        total = part_ref[pl.ds(mine, rows // 2), cols] + recv0[c].astype(wide)
+        half[c] = total.reshape(N_X, rows // 8, chunk)
+        send1[c] = total.astype(thin).reshape(N_X, rows // 8, chunk)
+        for k in range(1, N_X):
+            to = lax.rem(x + k, N_X)
+            send(c, k, send1.at[c, to], recv1.at[c, k - 1], at_x(k))
+
+    def step2(c):
+        arrive(c, range(1, 4))
+        total = half[c, x]
+        for k in range(3):
+            total = total + recv1[c, k].astype(wide)
+        half[c, 0] = total
+        send2[c] = total.astype(thin).reshape(N_Y, rows // 64, chunk)
+        for k in range(1, N_Y):
+            to = lax.rem(y + k, N_Y)
+            send(c, 3 + k, send2.at[c, to], recv2.at[c, k - 1], at_y(k))
+
+    def step3(c):
+        arrive(c, range(4, 11))
+        total = half[c, 0, pl.ds(pl.multiple_of(y * (rows // 64), rows // 64), rows // 64)]
+        for k in range(7):
+            total = total + recv2[c, k].astype(wide)
+        slots3[c, z] = total.astype(thin)
+        for k in range(1, N_Z):
+            send(c, 10 + k, slots3.at[c, z], slots3.at[c, z], at_z(k))
+
+    def step4(c):
+        arrive(c, range(11, 22))
+        total = slots3[c, 0].astype(wide)
+        for k in range(1, N_Z):
+            total = total + slots3[c, k].astype(wide)
+        fin4[c, y] = (total * (1.0 / 768)).astype(thin)
+        for k in range(1, N_Y):
+            send(c, 21 + k, fin4.at[c, y], fin4.at[c, y], at_y(k))
+
+    def step5(c):
+        arrive(c, range(22, 29))
+        fin5[c, x] = fin4[c].reshape(rows // 8, chunk)
+        for k in range(1, N_X):
+            send(c, 28 + k, fin5.at[c, x], fin5.at[c, x], at_x(k))
+
+    def step6(c):
+        arrive(c, range(29, 32))
+        fin6[c, core] = fin5[c].reshape(rows // 2, chunk)
+        send(c, 32, fin6.at[c, core], fin6.at[c, core], other_core)
+
+    def step7(c):
+        arrive(c, [32])
+        out_ref[:, c * chunk : (c + 1) * chunk] = fin6[c].reshape(rows, chunk)
+
+    steps = (step0, step1, step2, step3, step4, step5, step6, step7)
+    for wave in range(len(steps) + CHUNKS - 1):
+        for c in range(CHUNKS):
+            if 0 <= wave - c < len(steps):
+                steps[wave - c](c)
+
+
+def mean_over_devices(term):
+    rows, width = term.shape
+    chunk = width // CHUNKS
+    thin, wide = jnp.bfloat16, jnp.float32
+    eighth, block = rows // 8, rows // 64
+    mean = pl.pallas_call(
+        reduce_kernel,
+        out_shape=jax.ShapeDtypeStruct((rows, width), thin),
+        in_specs=[pl.BlockSpec(memory_space=pltpu.VMEM)],
+        out_specs=pl.BlockSpec(memory_space=pltpu.VMEM),
+        scratch_shapes=[
+            pltpu.VMEM((CHUNKS, rows // 2, chunk), thin),
+            pltpu.VMEM((CHUNKS, rows // 2, chunk), thin),
+            pltpu.VMEM((CHUNKS, N_X, eighth, chunk), wide),
+            pltpu.VMEM((CHUNKS, N_X, eighth, chunk), thin),
+            pltpu.VMEM((CHUNKS, N_X - 1, eighth, chunk), thin),
+            pltpu.VMEM((CHUNKS, N_Y, block, chunk), thin),
+            pltpu.VMEM((CHUNKS, N_Y - 1, block, chunk), thin),
+            pltpu.VMEM((CHUNKS, N_Z, block, chunk), thin),
+            pltpu.VMEM((CHUNKS, N_Y, block, chunk), thin),
+            pltpu.VMEM((CHUNKS, N_X, eighth, chunk), thin),
+            pltpu.VMEM((CHUNKS, N_CORE, rows // 2, chunk), thin),
+            pltpu.SemaphoreType.DMA((CHUNKS, 33)),
+            pltpu.SemaphoreType.DMA((CHUNKS, 33)),
+        ],
+        compiler_params=pltpu.CompilerParams(
+            collective_id=0, has_side_effects=True, vmem_limit_bytes=48 * 1024 * 1024
+        ),
+    )(term)
+    return mean.astype(wide)
 
 
 def pair_tables(count):
@@ -118,8 +274,7 @@
     grad_term = lax.dot_general(
         joined, pre_norm_grad, (((0,), (0,)), ((), ())), preferred_element_type=jnp.float32
     )
-    summed_grad = lax.psum(grad_term, ("shard", "rep"))
-    gcn_weight_grad = summed_grad / (peer_count * lax.axis_size("rep"))
+    gcn_weight_grad = mean_over_devices(grad_term)
     return (embeddings, embed_grad, click_logits, gcn_weight_grad)
 
 

time: 663 us -> 217 us (0.33)
  waiting for transfers between devices: 546 us -> 65.6 us
  Pallas kernels: 0 us -> 48.8 us
  between operations: 14.5 us -> 1.17 us
    psum x1 -> x0, waiting for transfers between devices: 477 us -> none  [on_device(): summed_grad = lax.psum(grad_term, ('shard', 'rep'))]
    pallas_call x0 -> x1, Pallas kernels: none -> 48.8 us  [mean_over_devices(): pl.pallas_call(reduce_kernel, out_shape=jax.ShapeDtypeStruct((rows, width...]
  transfers between devices with their start and end apart: 5 -> 4, of which waited for: 5 -> 4; matrix products, arithmetic and copies ran while one was open for 1% -> 4% of each run, Pallas kernels for 0% -> 0%
where the time goes in v1:
time: 217 us; the launch traced here: 216 us
  waiting for transfers between devices  65.6 us (30%)
  local copies, waits for them, and re-layouts  48.8 us (22%)
  Pallas kernels  48.8 us (22%)
  starting transfers between devices  25.7 us (12%)
  other arithmetic  18.1 us (8%)
  matrix products  7.44 us (3%)
    pallas_call x1, Pallas kernels, mean_over_devices(): pl.pallas_call(reduce_kernel, out_shape=jax.ShapeDtypeStruct((rows, width...  48.8 us
    all_to_all x1, waiting for transfers between devices, on_device(): lax.all_to_all(outboxes.reshape(peer_count, capacity, model_width), 'shar...  23.6 us
    all_to_all x1, waiting for transfers between devices, on_device(): lax.all_to_all(looked_up, 'shard', split_axis=0, concat_axis=0, tiled=True)  22.6 us
    gather x1, local copies, waits for them, and re-layouts, local_layer(): picked = tables[indices].astype(jnp.float32)  17.3 us
    all_to_all x1, waiting for transfers between devices, on_device(): lax.all_to_all(outgoing, 'shard', split_axis=0, concat_axis=0, tiled=True)  16.8 us
    all_to_all x1, starting transfers between devices, on_device(): lax.all_to_all(wanted, 'shard', split_axis=0, concat_axis=0, tiled=True)  13.8 us
    scatter-add x1, other arithmetic, on_device(): embed_grad = jnp.zeros((node_count, model_width), jnp.float32).at[asked.r...  7.31 us
    gather x1, local copies, waits for them, and re-layouts, on_device(): lower_grad[:, sym_table].reshape(requests, candidates + 1, candidates + 1)  6.54 us
  transfers between devices with their start and end apart: 4, of which 4 were waited for; matrix products, arithmetic and copies ran while one was open for 4% of the time, Pallas kernels for 0%

profile of v1, /device:TPU:1, one launch (start us, length us, event | category | flops | bytes accessed | tf_op | source)
XLA Modules:
  0.0 215.7 jit_solution(9144477177238351895)
XLA Ops:
  0.6 0.0 copy-start
  0.7 0.5 broadcast.237
  1.2 1.4 fusion.59
  2.6 0.1 eq.22
  2.7 1.2 reduce-window.6
  3.8 0.2 slice_reduce_fusion
  4.1 0.1 bitcast_bitcast_fusion
  4.2 0.1 mul.131
  4.3 0.8 reshape.260
  5.1 2.9 %scatter_custom_fusion = s32[896]{0:T(1024)S(1)} fusion(s32[400]{0:T(512)S(1)} %bitcast.50, s32[400]{0:T(512)S(1)} %reshape.260, s32[]{:T(128)} %constant.24.clone.1), kind=kCustom, calls=%fused_computation.87 | custom fusion | bytes 3588 | tf_op jit(solution)/shard_map/scatter | solution.py:220
  8.0 0.7 all_to_all.18
  8.7 13.8 %all-to-all-start.1 = ((s32[16,1,56]{2,1,0:T(1,128)}), s32[16,1,56]{2,1,0:T(1,128)S(1)}, u32[]{:S(2)}, u32[]{:S(2)}) async-start(s32[16,1,56]{2,1,0:T(1,128)} %all_to_all.18), calls=%async_computation.1 | async-start | bytes 16384 | tf_op jit(solution)/shard_map/all_to_all | solution.py:223
  22.5 0.8 reshape_squeeze.3
  23.2 3.6 %gather_fusion = bf16[512,512]{1,0:T(8,128)(2,1)} fusion(bf16[256,512]{1,0:T(8,128)(2,1)} %param.15, s32[1024]{0:T(1024)S(1)} %pad_clamp_fusion.4), kind=kCustom, calls=%fused_computation | custom fusion | bytes 1050624 | tf_op jit(solution)/shard_map/gather | solution.py:203
  26.9 2.6 %all-to-all-done.1 = s32[16,1,56]{2,1,0:T(1,128)S(1)} async-done(((s32[16,1,56]{2,1,0:T(1,128)}), s32[16,1,56]{2,1,0:T(1,128)S(1)}, u32[]{:S(2)}, u32[]{:S(2)}) %all-to-all-start.1) | async-done | bytes 3616 | tf_op jit(solution)/shard_map/all_to_all | solution.py:223
  29.4 4.7 %all-to-all-start = ((bf16[16,32,512]{2,1,0:T(8,128)(2,1)}), bf16[16,32,512]{2,1,0:T(8,128)(2,1)S(1)}, u32[]{:S(2)}, u32[]{:S(2)}) async-start(bf16[16,32,512]{2,1,0:T(8,128)(2,1)} %bitcast.1), calls=%async_computation | async-start | bytes 1048576 | tf_op jit(solution)/shard_map/all_to_all | solution.py:204
  34.2 0.1 copy.34
  34.3 0.1 reshape.218
  34.4 0.1 copy.33
  34.5 0.1 reshape.226
  34.6 16.8 %all-to-all-done = bf16[16,32,512]{2,1,0:T(8,128)(2,1)S(1)} async-done(((bf16[16,32,512]{2,1,0:T(8,128)(2,1)}), bf16[16,32,512]{2,1,0:T(8,128)(2,1)S(1)}, u32[]{:S(2)}, u32[]{:S(2)}) %all-to-all-start) | async-done | bytes 524320 | tf_op jit(solution)/shard_map/all_to_all | solution.py:204
  51.5 0.1 pad_maximum_fusion
  51.5 17.3 %gather_fusion.1 = bf16[4096,512]{1,0:T(8,128)(2,1)} fusion(bf16[768,512]{1,0:T(8,128)(2,1)S(1)} %pad_maximum_fusion, s32[4096]{0:T(1024)S(1)} %broadcast_clamp_fusion), kind=kCustom, calls=%fused_computation.1 | custom fusion | bytes 8404992 | tf_op jit(solution)/shard_map/gather | solution.py:180
  68.8 3.5 %fusion = f32[256,512]{1,0:T(8,128)S(1)} fusion(f32[256,16]{1,0:T(8,128)S(1)} %copy.33, bf16[4096,512]{1,0:T(8,128)(2,1)} %gather_fusion.1), kind=kLoop, calls=%fused_computation.10 | loop fusion | flops 6160384 | bytes 4734976 | tf_op jit(solution)/shard_map/reduce_sum | solution.py:181
  72.3 0.1 divide_convert_fusion
  72.4 0.5 multiply_reduce_fusion.1
  72.9 0.6 copy-done.18
  73.5 0.1 multiply_convert_fusion
  73.7 0.0 copy-start.17
  73.7 0.0 copy-start.13
  73.7 4.0 %gather_fusion.2 = bf16[896,512]{1,0:T(8,128)(2,1)} fusion(bf16[256,512]{1,0:T(8,128)(2,1)S(1)} %multiply_convert_fusion, s32[1024]{0:T(1024)S(1)} %pad_clamp_fusion.3), kind=kCustom, calls=%fused_computation.2 | custom fusion | bytes 1838592 | tf_op jit(solution)/shard_map/gather | solution.py:224
  77.7 3.7 %all-to-all-start.2 = ((bf16[16,56,512]{2,1,0:T(8,128)(2,1)}), bf16[16,56,512]{2,1,0:T(8,128)(2,1)S(1)}, u32[]{:S(2)}, u32[]{:S(2)}) async-start(bf16[16,56,512]{2,1,0:T(8,128)(2,1)} %bitcast.43), calls=%async_computation.2 | async-start | bytes 1835008 | tf_op jit(solution)/shard_map/all_to_all | solution.py:225
  81.4 0.6 convert_element_type.45
  82.0 0.6 pad_clamp_fusion.1
  82.7 0.6 pad_clamp_fusion
  83.3 22.6 %all-to-all-done.2 = bf16[16,56,512]{2,1,0:T(8,128)(2,1)S(1)} async-done(((bf16[16,56,512]{2,1,0:T(8,128)(2,1)}), bf16[16,56,512]{2,1,0:T(8,128)(2,1)S(1)}, u32[]{:S(2)}, u32[]{:S(2)}) %all-to-all-start.2) | async-done | bytes 917536 | tf_op jit(solution)/shard_map/all_to_all | solution.py:225
  105.9 2.1 gather_fusion.3
  107.9 0.1 reshape.202
  108.1 0.3 convolution_multiply_fusion
  108.4 0.2 reshape.203
  108.6 0.4 copy.38
  108.9 3.2 %gather_fusion.4 = bf16[1275,8]{1,0:T(8,128)(2,1)S(1)} fusion(bf16[8,2601]{0,1:T(8,128)(2,1)S(1)} %copy.38, s32[2048]{0:T(1024)} %pad_clamp_fusion.1), kind=kCustom, calls=%fused_computation.4 | custom fusion | bytes 45900 | tf_op jit(solution)/shard_map/gather | solution.py:233
  112.2 0.1 copy.39
  112.3 2.8 %fusion.27 = f32[8,1024]{1,0:T(8,128)S(1)} fusion(bf16[1787,1024]{1,0:T(8,128)(2,1)} %param.23, bf16[8,1275]{1,0:T(8,128)(2,1)S(1)} %copy.39, bf16[8,512]{1,0:T(8,128)(2,1)} %param.20), kind=kOutput, calls=%fused_computation.63 | convolution fusion | flops 29335392 | bytes 3721136 | tf_op jit(solution)/shard_map/dot_general | solution.py:235
  115.1 0.4 copy-done.4
  115.5 1.6 fusion.1
  117.1 0.1 concatenate.19.clone
  117.2 6.5 %gather_fusion.5 = bf16[2601,8]{1,0:T(8,128)(2,1)S(1)} fusion(bf16[8,1276]{0,1:T(8,128)(2,1)S(1)} %concatenate.19.clone, s32[3072]{0:T(1024)} %pad_clamp_fusion), kind=kCustom, calls=%fused_computation.5 | custom fusion | bytes 93636 | tf_op jit(solution)/shard_map/gather | solution.py:249
  123.7 0.2 copy.41
  124.0 0.2 convert_element_type.49
  124.1 1.0 fusion.11
  125.2 0.1 fusion.5
  125.3 0.1 reshape.268
  125.4 3.1 %scatter_custom_fusion.1 = bf16[896,512]{1,0:T(8,128)(2,1)} fusion(s32[400]{0:T(512)} %bitcast.52, bf16[400,512]{1,0:T(8,128)(2,1)S(1)} %reshape.268, bf16[]{:T(256)} %constant.14.clone.1), kind=kCustom, calls=%fused_computation.29 | custom fusion | bytes 918016 | tf_op jit(solution)/shard_map/scatter | solution.py:258
  128.6 3.5 %all-to-all-start.3 = ((bf16[16,56,512]{2,1,0:T(8,128)(2,1)}), bf16[16,56,512]{2,1,0:T(8,128)(2,1)S(1)}, u32[]{:S(2)}, u32[]{:S(2)}) async-start(bf16[16,56,512]{2,1,0:T(8,128)(2,1)} %bitcast.13), calls=%async_computation.3 | async-start | bytes 1835008 | tf_op jit(solution)/shard_map/all_to_all | solution.py:260
  132.2 0.7 reduce.15
  132.8 0.1 reshape.200
  133.0 0.6 convolution_bitcast_fusion
  133.6 23.6 %all-to-all-done.3 = bf16[16,56,512]{2,1,0:T(8,128)(2,1)S(1)} async-done(((bf16[16,56,512]{2,1,0:T(8,128)(2,1)}), bf16[16,56,512]{2,1,0:T(8,128)(2,1)S(1)}, u32[]{:S(2)}, u32[]{:S(2)}) %all-to-all-start.3) | async-done | bytes 917536 | tf_op jit(solution)/shard_map/all_to_all | solution.py:260
  157.2 7.3 %scatter_custom_fusion.2 = f32[256,512]{1,0:T(8,128)S(1)} fusion(s32[896]{0:T(1024)S(1)} %fusion.40, bf16[896,512]{1,0:T(8,128)(2,1)S(1)} %bitcast.44, f32[]{:T(128)} %constant.27.clone.1), kind=kCustom, calls=%fused_computation.13 | custom fusion | flops 917504 | bytes 1441796 | tf_op jit(solution)/shard_map/scatter-add | solution.py:270
  164.6 0.1 multiply_reduce_fusion
  164.7 0.6 fusion.9.part_ref
  165.3 48.8 %shard_map.174 = bf16[1024,512]{1,0:T(8,128)(2,1)S(1)} custom-call(f32[1024,512]{1,0:T(8,128)S(1)} %fusion.9.part_ref), custom_call_target="tpu_custom_call" | custom-call | tf_op jit(solution)/shard_map/pallas_call | solution.py:139
  214.1 1.6 convert_element_type.54
  (57 shorter events, 0.3 us)
Async XLA Ops:
  0.6 71.8 %copy-start = (bf16[1024,512]{1,0:T(8,128)(2,1)S(1)}, bf16[1024,512]{1,0:T(8,128)(2,1)}, u32[]{:S(2)}) copy-start(bf16[1024,512]{1,0:T(8,128)(2,1)} %param.19) | copy-start | bytes 3145732
  0.6 50.8 %copy-start.2 = (bf16[256,512]{1,0:T(8,128)(2,1)S(1)}, bf16[256,512]{1,0:T(8,128)(2,1)}, u32[]{:S(2)}) copy-start(bf16[256,512]{1,0:T(8,128)(2,1)} %param.15) | copy-start | bytes 786436
  0.7 33.5 %copy-start.12 = (s32[256,16]{0,1:T(8,128)S(1)}, s32[256,16]{0,1:T(8,128)}, u32[]{:S(2)}) copy-start(s32[256,16]{0,1:T(8,128)} %param.17) | copy-start | bytes 49156
  0.7 33.7 %copy-start.8 = (f32[256,16]{0,1:T(8,128)S(1)}, f32[256,16]{0,1:T(8,128)}, u32[]{:S(2)}) copy-start(f32[256,16]{0,1:T(8,128)} %param.18) | copy-start | bytes 49156
  5.0 77.0 %copy-start.16 = (s32[400,1]{0,1:T(1,128)}, s32[400,1]{0,1:T(1,128)S(1)}, u32[]{:S(2)}) copy-start(s32[400,1]{0,1:T(1,128)S(1)} %compare_select_fusion.3) | copy-start | bytes 4804
  8.7 20.8 %all-to-all-start.1 = ((s32[16,1,56]{2,1,0:T(1,128)}), s32[16,1,56]{2,1,0:T(1,128)S(1)}, u32[]{:S(2)}, u32[]{:S(2)}) async-start(s32[16,1,56]{2,1,0:T(1,128)} %all_to_all.18), calls=%async_computation.1 | async-start | bytes 16384 | tf_op jit(solution)/shard_map/all_to_all | solution.py:223
  29.4 22.0 %copy-start.5 = (s32[16,1,56]{2,1,0:T(1,128)}, s32[16,1,56]{2,1,0:T(1,128)S(1)}, u32[]{:S(2)}) copy-start(s32[16,1,56]{2,1,0:T(1,128)S(1)} %all-to-all-done.1) | copy-start | bytes 10756
  29.4 22.0 %all-to-all-start = ((bf16[16,32,512]{2,1,0:T(8,128)(2,1)}), bf16[16,32,512]{2,1,0:T(8,128)(2,1)S(1)}, u32[]{:S(2)}, u32[]{:S(2)}) async-start(bf16[16,32,512]{2,1,0:T(8,128)(2,1)} %bitcast.1), calls=%async_computation | async-start | bytes 1048576 | tf_op jit(solution)/shard_map/all_to_all | solution.py:204
  72.9 0.6 copy-start.18
  73.6 4.0 %copy-start.1 = (bf16[256,512]{1,0:T(8,128)(2,1)}, bf16[256,512]{1,0:T(8,128)(2,1)S(1)}, u32[]{:S(2)}) copy-start(bf16[256,512]{1,0:T(8,128)(2,1)S(1)} %multiply_convert_fusion) | copy-start | bytes 786436
  73.6 7.8 %copy-start.11 = (bf16[8,512]{1,0:T(8,128)(2,1)S(1)}, bf16[8,512]{1,0:T(8,128)(2,1)}, u32[]{:S(2)}) copy-start(bf16[8,512]{1,0:T(8,128)(2,1)} %param.20) | copy-start | bytes 24580
  73.6 7.8 %copy-start.14 = (bf16[1024]{0:T(1024)(128)(2,1)S(1)}, bf16[1024]{0:T(1024)(128)(2,1)}, u32[]{:S(2)}) copy-start(bf16[1024]{0:T(1024)(128)(2,1)} %param.24) | copy-start | bytes 6148
  73.7 8.4 %copy-start.17 = (s32[1275]{0:T(1024)S(1)}, s32[1275]{0:T(1024)}, u32[]{:S(2)}) copy-start(s32[1275]{0:T(1024)} %constant.86) | copy-start | bytes 15304
  73.7 9.0 %copy-start.13 = (s32[2601]{0:T(1024)S(1)}, s32[2601]{0:T(1024)}, u32[]{:S(2)}) copy-start(s32[2601]{0:T(1024)} %constant.87) | copy-start | bytes 31216
  77.7 28.2 %all-to-all-start.2 = ((bf16[16,56,512]{2,1,0:T(8,128)(2,1)}), bf16[16,56,512]{2,1,0:T(8,128)(2,1)S(1)}, u32[]{:S(2)}, u32[]{:S(2)}) async-start(bf16[16,56,512]{2,1,0:T(8,128)(2,1)} %bitcast.43), calls=%async_computation.2 | async-start | bytes 1835008 | tf_op jit(solution)/shard_map/all_to_all | solution.py:225
  81.4 27.1 %copy-start.7 = (bf16[8,1,512]{2,1,0:T(2,128)(2,1)}, bf16[8,1,512]{2,1,0:T(2,128)(2,1)S(1)}, u32[]{:S(2)}) copy-start(bf16[8,1,512]{2,1,0:T(2,128)(2,1)S(1)} %copy.37) | copy-start | bytes 24580
  112.2 3.0 %copy-start.20 = (f32[1024]{0:T(1024)S(1)}, f32[1024]{0:T(1024)}, u32[]{:S(2)}) copy-start(f32[1024]{0:T(1024)} %convert_element_type.45) | copy-start | bytes 12292
  112.3 3.2 %copy-start.4 = (bf16[1787,1024]{1,0:T(8,128)(2,1)S(1)}, bf16[1787,1024]{1,0:T(8,128)(2,1)}, u32[]{:S(2)}) copy-start(bf16[1787,1024]{1,0:T(8,128)(2,1)} %param.23) | copy-start | bytes 10979332
  115.5 1.6 copy-start.9
  123.9 8.2 %copy-start.15 = (bf16[1024]{0:T(1024)(128)(2,1)S(1)}, bf16[1024]{0:T(1024)(128)(2,1)}, u32[]{:S(2)}) copy-start(bf16[1024]{0:T(1024)(128)(2,1)} %param.24) | copy-start | bytes 6148
  124.0 8.2 %copy-start.6 = (s32[16,1,56]{2,1,0:T(1,128)S(1)}, s32[16,1,56]{2,1,0:T(1,128)}, u32[]{:S(2)}) copy-start(s32[16,1,56]{2,1,0:T(1,128)} %copy-done.5) | copy-start | bytes 10756
  124.0 9.0 %copy-start.10 = (f32[8,1024]{1,0:T(8,128)S(1)}, f32[8,1024]{1,0:T(8,128)}, u32[]{:S(2)}) copy-start(f32[8,1024]{1,0:T(8,128)} %copy-done.9) | copy-start | bytes 98308
  125.2 39.5 %copy-start.19 = (f32[256]{0:T(256)S(1)}, f32[256]{0:T(256)}, u32[]{:S(2)}) copy-start(f32[256]{0:T(256)} %copy-done.18) | copy-start | bytes 3076
  128.6 28.6 %all-to-all-start.3 = ((bf16[16,56,512]{2,1,0:T(8,128)(2,1)}), bf16[16,56,512]{2,1,0:T(8,128)(2,1)S(1)}, u32[]{:S(2)}, u32[]{:S(2)}) async-start(bf16[16,56,512]{2,1,0:T(8,128)(2,1)} %bitcast.13), calls=%async_computation.3 | async-start | bytes 1835008 | tf_op jit(solution)/shard_map/all_to_all | solution.py:260
  164.6 49.5 %copy-start.3 = (f32[256,512]{1,0:T(8,128)}, f32[256,512]{1,0:T(8,128)S(1)}, u32[]{:S(2)}) copy-start(f32[256,512]{1,0:T(8,128)S(1)} %scatter_custom_fusion.2) | copy-start | bytes 1572868

commit v2 on v0

v2 whole, which is shorter than its diff:
```python
import math

import jax
import jax.numpy as jnp
from jax import lax
from jax.experimental import pallas as pl
from jax.experimental.pallas import tpu as pltpu
from jax.sharding import PartitionSpec as P

MESH = pl.DeviceIdType.MESH
F32, BF16, I32, I16 = jnp.float32, jnp.bfloat16, jnp.int32, jnp.int16
N_X, N_Y, N_Z, GROUP = 4, 8, 12, 16
NODES, WIDTH, DEG, BND = 256, 512, 16, 32
REQS, CAND, PAD, CAP = 8, 50, 64, 56
SLOTS = REQS * PAD
PAIRS = CAND * (CAND + 1) // 2
CHUNKS = 2
ROOT = 1.0 / math.sqrt(WIDTH)


def mm(a, b):
    return lax.dot_general(a, b, (((1,), (0,)), ((), ())), preferred_element_type=F32)


def nt(a, b):
    return lax.dot_general(a, b, (((1,), (1,)), ((), ())), preferred_element_type=F32)


def tn(a, b):
    return lax.dot_general(a, b, (((0,), (0,)), ((), ())), preferred_element_type=F32)


def iota(shape, axis):
    return lax.broadcasted_iota(I32, shape, axis)


def mark(condition):
    return jnp.where(condition, 1.0, 0.0).astype(BF16)


def rows_at(start, count, unit):
    return pl.ds(pl.multiple_of(start, unit), count)


def wide(column, times):
    return jnp.concatenate([column] * times, axis=1)


def kernel(
    feats,
    send_rows,
    neighbors,
    weights,
    gcn_hbm,
    user,
    owners,
    wanted,
    mlp_hbm,
    out_weight,
    logit_grad,
    emb_out,
    grad_out,
    click_out,
    mean_out,
    meta,
    table,
    owner_b,
    row_b,
    place,
    msg_out,
    msg_in,
    cid,
    gid,
    wgt,
    wsum,
    picks,
    mix,
    halo_pick,
    halo,
    own_id,
    own_w,
    own_mix,
    acc,
    joined,
    unit,
    inv,
    stack,
    grams,
    lower,
    pair_grad,
    cand_grad,
    pre_grad,
    term,
    outbox,
    inbox,
    spread,
    mlp,
    gcn,
    send0,
    recv0,
    half,
    send1,
    recv1,
    send2,
    recv2,
    slots3,
    fin4,
    fin5,
    fin6,
    w_sem,
    meta_s,
    meta_r,
    metac_s,
    metac_r,
    feat_s,
    feat_r,
    featc_s,
    featc_r,
    msg_s,
    msg_r,
    box_s,
    box_r,
    red_s,
    red_r,
):
    shard, rep = lax.axis_index("shard"), lax.axis_index("rep")
    y, core = lax.div(shard, 2), lax.rem(shard, 2)
    z, x = lax.div(rep, N_X), lax.rem(rep, N_X)
    me = shard

    def at_shard(k):
        return {"shard": lax.rem(shard + k, GROUP)}

    def at_x(k):
        return {"rep": z * N_X + lax.rem(x + k, N_X)}

    def at_y(k):
        return {"shard": lax.rem(y + k, N_Y) * 2 + core}

    def at_z(k):
        return {"rep": lax.rem(z + k, N_Z) * N_X + x}

    other_core = {"shard": y * 2 + 1 - core}
    right, left = at_y(1), at_y(N_Y - 1)

    peers = [at_shard(k) for k in range(1, GROUP)]
    peers += [at_x(k) for k in range(1, N_X)] + [at_z(k) for k in range(1, N_Z)]
    barrier = pltpu.get_barrier_semaphore()
    for peer in peers:
        pl.semaphore_signal(barrier, inc=1, device_id=peer, device_id_type=MESH)

    local = [
        pltpu.make_async_copy(gcn_hbm, gcn, w_sem.at[0]),
        pltpu.make_async_copy(mlp_hbm, mlp, w_sem.at[1]),
    ]
    for copy in local:
        copy.start()

    sent = []

    def send(src, dst, s_sem, r_sem, peer):
        copy = pltpu.make_async_remote_copy(
            src_ref=src,
            dst_ref=dst,
            send_sem=s_sem,
            recv_sem=r_sem,
            device_id=peer,
            device_id_type=MESH,
        )
        copy.start()
        sent.append(copy)
        return copy

    ids = neighbors[...]
    id_hi = lax.shift_right_logical(ids, 8).astype(F32).astype(BF16)
    id_lo = jnp.bitwise_and(ids, 255).astype(F32).astype(BF16)
    w_own = weights[...].astype(BF16)

    def put(values, offset):
        return mm(values, mark(iota((DEG, 128), 1) == iota((DEG, 128), 0) + offset))

    packed = jnp.zeros((128, 128), F32)
    for part in range(2):
        cut = slice(part * 128, part * 128 + 128)
        base = part * 64
        packed = packed + put(id_hi[cut], base) + put(id_lo[cut], base + 16) + put(w_own[cut], base + 32)
    meta[me, 0:128, :] = packed.astype(BF16)
    sr = send_rows[0].astype(F32).astype(BF16)
    meta[me, 128:144, :] = mm(sr, mark(iota((BND, 128), 1) == iota((BND, 128), 0))).astype(BF16)
    table[y, rows_at(core * NODES, NODES, NODES), :] = feats[...]

    pl.semaphore_wait(barrier, len(peers))

    def chip(d):
        return lax.rem(y + d + N_Y, N_Y)

    meta_got, metac_got, feat_got, featc_got = {}, {}, {}, {}

    def meta_ring(way, hop):
        block = chip(-hop if way == 0 else hop) * 2 + core
        ref = meta.at[block]
        number = way * 4 + hop
        meta_got[way, hop] = send(
            ref, ref, meta_s.at[number], meta_r.at[number], right if way == 0 else left
        )

    def meta_core(d, number):
        ref = meta.at[chip(d) * 2 + core]
        metac_got[d] = send(ref, ref, metac_s.at[number], metac_r.at[number], other_core)

    def feat_ref(d, part):
        return table.at[chip(d), rows_at(core * NODES + part * 128, 128, 128)]

    def feat_ring(way, hop, part):
        ref = feat_ref(-hop if way == 0 else hop, part)
        number = (way * 4 + hop) * 2 + part
        feat_got[way, hop, part] = send(
            ref, ref, feat_s.at[number], feat_r.at[number], right if way == 0 else left
        )

    core_order = (0, -1, 1, -2, 2, -3, 3, 4)

    def feat_core(d, part):
        number = core_order.index(d) * 2 + part
        ref = feat_ref(d, part)
        featc_got[d, part] = send(ref, ref, featc_s.at[number], featc_r.at[number], other_core)

    def meta_step(hop):
        meta_got[0, hop].wait_recv()
        if hop < 3:
            meta_ring(0, hop + 1)
            meta_got[1, hop].wait_recv()
            if hop < 2:
                meta_ring(1, hop + 1)
            meta_core(-1 - hop, 1 + 2 * hop)
            meta_core(1 + hop, 2 + 2 * hop)
        else:
            meta_core(4, 7)

    def feat_step(hop, part):
        if hop < 3:
            feat_got[0, hop, part].wait_recv()
            if hop < 2 or part == 0:
                feat_ring(0, hop + 1, part)
            feat_got[1, hop, part].wait_recv()
            if hop < 2 or part == 1:
                feat_ring(1, hop + 1, part)
            feat_core(-1 - hop, part)
            feat_core(1 + hop, part)
        else:
            feat_got[part, hop, part].wait_recv()
            feat_core(4, part)

    meta_ring(0, 0)
    meta_ring(1, 0)
    meta_core(0, 0)
    for part in range(2):
        feat_ring(0, 0, part)
        feat_ring(1, 0, part)
    for part in range(2):
        feat_core(0, part)

    request = lax.shift_right_logical(iota((SLOTS, REQS), 0), 6)
    of_request = mark(request == iota((SLOTS, REQS), 1))
    within = jnp.bitwise_and(iota((SLOTS, CAND), 0), PAD - 1)
    hit = iota((SLOTS, CAND), 1) == within - 1
    spot = jnp.bitwise_and(iota((SLOTS, 128), 0), PAD - 1)
    valid = (spot >= 1) & (spot <= CAND)

    def column(values):
        spread_out = mm(of_request, values.astype(F32).astype(BF16))
        return mm(jnp.where(hit, spread_out, 0.0).astype(BF16), jnp.ones((CAND, 128), BF16))

    owner_col = jnp.where(valid, column(owners[...]), -1.0)
    row_col = jnp.where(valid, column(wanted[...]), 0.0)
    owner_b[...] = owner_col
    row_b[...] = row_col
    cid[...] = jnp.where(valid, owner_col * NODES + row_col, -1.0).astype(I32).astype(I16)

    meta_step(0)

    lanes = iota((SLOTS, 128), 1).astype(F32)
    hits = mark(owner_col == lanes)
    below = mark(iota((SLOTS, SLOTS), 0) >= iota((SLOTS, SLOTS), 1))
    counts = mm(below, hits)
    rank = mm((jnp.where(owner_col == lanes, counts, 0.0)).astype(BF16), jnp.ones((128, 128), BF16))
    slot_col = jnp.where(valid, owner_col * 128 + rank - 1.0, -4096.0)
    slot_lane = slot_col.T[0:16, :]
    row_lane = row_col.T[0:16, :].astype(BF16)

    meta_step(1)

    def place_owner(owner, carry):
        mine = slot_lane[0:1, :] - owner.astype(F32) * 128
        at = iota((128, SLOTS), 0)
        at = jnp.where(at >= CAP, at - CAP, at)
        at = jnp.where(iota((128, SLOTS), 0) >= 2 * CAP, -30000, at)
        chosen = mark(at.astype(F32) == mine)
        place[owner] = chosen
        msg_out[owner] = nt(row_lane, chosen).astype(BF16)
        return carry

    lax.fori_loop(0, GROUP, place_owner, 0)
    meta_step(2)
    msg_in[me] = msg_out[me]
    msg_got = []
    for k in range(1, GROUP):
        to = lax.rem(me + k, GROUP)
        msg_got.append(send(msg_out.at[to], msg_in.at[me], msg_s.at[k - 1], msg_r.at[k - 1], at_shard(k)))
    feat_step(0, 0)

    w_own_sum = mm(w_own, jnp.ones((DEG, 128), BF16))

    def own_k(k, carry):
        pick = mark(iota((DEG, 128), 0) == k)
        own_id[k] = (mm(id_hi, pick) * 256 + mm(id_lo, pick)).astype(I32).astype(I16)
        own_w[k] = mm(w_own, pick).astype(BF16)
        return carry

    lax.fori_loop(0, DEG, own_k, 0)

    def own_rows(tile, carry):
        rows = rows_at(tile * 16, 16, 16)
        found = [own_id[k, rows, :] for k in range(DEG)]
        share = [own_w[k, rows, :] for k in range(DEG)]
        for t in range(6):
            lane = (iota((16, 128), 1) + t * 128).astype(I16)
            total = jnp.zeros((16, 128), BF16)
            for k in range(DEG):
                total = total + jnp.where(found[k] == lane, share[k], jnp.zeros((16, 128), BF16))
            own_mix[rows, t * 128 : t * 128 + 128] = total
        return carry

    lax.fori_loop(0, NODES // 16, own_rows, 0)

    meta_step(3)
    for d in core_order:
        metac_got[d].wait_recv()
    feat_step(0, 1)

    narrow = jnp.where(row_b[...] >= 128, row_b[...] - 128, row_b[...])
    meta_id = jnp.where(valid, owner_b[...] * 128 + narrow, -1.0)

    def meta_pick(p, total):
        chosen = mark(meta_id == (iota((SLOTS, 128), 1) + p * 128).astype(F32))
        return total + mm(chosen, meta[p, 0:128, :])

    got = lax.fori_loop(0, GROUP, meta_pick, jnp.zeros((SLOTS, 128), F32))
    got = jnp.where(row_b[...] >= 128, pltpu.roll(got, 64, 1), got)
    lane128 = iota((SLOTS, 128), 1)
    got = jnp.where(lane128 < 48, got, 0.0).astype(BF16)
    wsum[...] = mm(got, mark(iota((128, 128), 0) >= 32))

    owner16 = mark(owner_b[:, 0:GROUP] == iota((SLOTS, GROUP), 1).astype(F32))
    mine16 = mark(iota((GROUP, 128), 0) == me)
    for j in range(4):
        tile = jnp.zeros((GROUP, 128), F32)
        for i in range(4):
            rows = meta[4 * j + i, 128:144, :].astype(F32)
            tile = tile + (pltpu.roll(rows, 32 * i, 1) if i else rows)
        tile = tile.astype(BF16)
        picks[:, j * 128 : j * 128 + 128] = mm(owner16, tile).astype(BF16)
        from_me = tn(tile, mine16)
        odd = jnp.bitwise_and(lax.shift_right_logical(iota((128, 128), 0), 5), 1).astype(F32)
        from_me = from_me + odd * NODES
        for t in range(4):
            lane = (iota((128, 128), 1) + t * 128).astype(F32)
            halo_pick[j * 128 : j * 128 + 128, t * 128 : t * 128 + 128] = mark(from_me == lane)

    def cand_k(k, carry):
        spots = iota((128, 128), 0)
        hi = mm(got, mark(spots == k))
        lo = mm(got, mark(spots == k + 16))
        wgt[k] = mm(got, mark(spots == k + 32)).astype(BF16)
        ext = hi * 256 + lo - 256
        ext16 = ext.astype(I32).astype(I16)
        found = jnp.zeros((SLOTS, 128), BF16)
        for j in range(4):
            lane = (iota((SLOTS, 128), 1) + j * 128).astype(I16)
            found = found + jnp.where(
                ext16 == lane, picks[:, j * 128 : j * 128 + 128], jnp.zeros((SLOTS, 128), BF16)
            )
        far = mm(found, jnp.ones((128, 128), BF16))
        source = jnp.floor(ext * (1.0 / BND))
        where = jnp.where(hi < 0.5, owner_b[...] * NODES + lo, source * NODES + far)
        gid[k] = where.astype(I32).astype(I16)
        return carry

    lax.fori_loop(0, DEG, cand_k, 0)
    feat_step(1, 0)

    def build(d):
        block = chip(d)

        def rows_of(tile, carry):
            rows = rows_at(tile * 16, 16, 16)
            found = [gid[k, rows, :] for k in range(DEG)]
            share = [wgt[k, rows, :] for k in range(DEG)]
            itself = cid[rows, :]
            nothing = jnp.zeros((16, 128), BF16)
            for t in range(4):
                lane = (iota((16, 128), 1) + (block * 512 + t * 128)).astype(I16)
                cols = slice(t * 128, t * 128 + 128)
                total = nothing
                for k in range(DEG):
                    total = total + jnp.where(found[k] == lane, share[k], nothing)
                mix[block, rows, cols] = jnp.where(itself == lane, jnp.ones((16, 128), BF16), nothing)
                mix[block, rows_at(SLOTS + tile * 16, 16, 16), cols] = total
            return carry

        lax.fori_loop(0, SLOTS // 16, rows_of, 0)

    def absorb(d, first=False):
        block = chip(d)
        for part in range(2):
            featc_got[d, part].wait_recv()

        def rows_of(tile, carry):
            rows = rows_at(tile * 256, 256, 256)
            product = mm(mix[block, rows, :], table[block])
            acc[rows, :] = product if first else acc[rows, :] + product
            return carry

        lax.fori_loop(0, 2 * SLOTS // 256, rows_of, 0)
        pick = rows_at(block * 64, 64, 64)
        halo[pick, :] = mm(halo_pick[pick, :], table[block]).astype(BF16)

    build(0)
    absorb(0, True)
    feat_step(1, 1)
    build(-1)
    absorb(-1)
    build(1)
    absorb(1)
    feat_step(2, 0)
    build(-2)
    build(2)
    feat_step(2, 1)
    absorb(-2)
    absorb(2)
    build(-3)
    build(3)
    build(4)
    feat_step(3, 0)
    feat_step(3, 1)
    absorb(-3)
    absorb(3)
    absorb(4)

    local[0].wait()

    def embed(tile, carry):
        rows = rows_at(tile * 256, 256, 256)
        sums = wsum[rows, :]
        scale = 1.0 / jnp.where(sums > 0, sums, 1.0)
        itself = acc[rows, :].astype(BF16)
        around = (acc[rows_at(SLOTS + tile * 256, 256, 256), :] * wide(scale, 4)).astype(BF16)
        joined[rows, 0:WIDTH] = itself
        joined[rows, WIDTH:] = around
        projected = mm(itself, gcn[0:WIDTH, :]) + mm(around, gcn[WIDTH:, :])
        root = lax.rsqrt(jnp.mean(projected * projected, axis=-1, keepdims=True) + 1e-06)
        ready = projected * root
        unit[rows, :] = ready
        inv[rows, :] = jnp.broadcast_to(root, (256, 128))
        line = iota((256, REQS), 0) + tile * 256
        users = mm(mark(lax.shift_right_logical(line, 6) == iota((256, REQS), 1)), user[...])
        is_user = jnp.bitwise_and(iota((256, WIDTH), 0), PAD - 1) == 0
        stack[rows, :] = jnp.where(is_user, users, ready).astype(BF16)
        return carry

    lax.fori_loop(0, SLOTS // 256, embed, 0)
    stack[SLOTS : SLOTS + PAD, :] = jnp.zeros((PAD, WIDTH), BF16)

    def gram(q, carry):
        grams[q] = nt(stack[rows_at(q * PAD, PAD, PAD), :], stack[rows_at(q * PAD, 2 * PAD, PAD), :]) * ROOT
        return carry

    lax.fori_loop(0, REQS, gram, 0)

    lane8 = iota((REQS, 128), 1)
    strips = [jnp.zeros((REQS, 128), F32) for _ in range(PAIRS // 128 + 2)]
    for i in range(1, CAND + 1):
        strip, shift = divmod(i * (i - 1) // 2, 128)
        line = jnp.where(lane8 < i, grams[:, i, :], 0.0)
        if shift:
            line = pltpu.roll(line, shift, 1)
        if shift + i > 128:
            strips[strip] = strips[strip] + jnp.where(lane8 >= shift, line, 0.0)
            strips[strip + 1] = strips[strip + 1] + jnp.where(lane8 < shift, line, 0.0)
        else:
            strips[strip] = strips[strip] + line
    whole = PAIRS // 128 * 128
    pairs = jnp.concatenate(strips[: PAIRS // 128], axis=1).astype(BF16)
    tail = strips[PAIRS // 128][:, 0 : PAIRS - whole].astype(BF16)

    local[1].wait()
    split = WIDTH + whole
    pre = mm(user[...], mlp[0:WIDTH, :]) + mm(pairs, mlp[WIDTH:split, :])
    pre = pre + mm(tail, mlp[split : WIDTH + PAIRS, :])
    bend = math.sqrt(2.0 / math.pi)
    curve = jnp.tanh(bend * (pre + 0.044715 * (pre * pre * pre)))
    hidden = (pre * (0.5 * (1.0 + curve))).astype(BF16).astype(F32)
    out_w = out_weight[...].astype(F32)
    click = jnp.sum(hidden * out_w, axis=1, keepdims=True)
    click_out[...] = jnp.broadcast_to(click, (REQS, 128))
    slope = 0.5 * (1.0 + curve) + 0.5 * pre * (1.0 - curve * curve) * bend * (1.0 + 3 * 0.044715 * pre * pre)
    hidden_grad = (logit_grad[...] * out_w * slope).astype(BF16)
    pair_grad[:, whole:] = jnp.zeros((REQS, 128), F32)
    pair_grad[:, 0:whole] = nt(hidden_grad, mlp[WIDTH:split, :])
    pair_grad[:, whole:PAIRS] = nt(hidden_grad, mlp[split : WIDTH + PAIRS, :])

    lower[...] = jnp.zeros((REQS, PAD, 128), F32)
    for i in range(1, CAND + 1):
        strip, shift = divmod(i * (i - 1) // 2, 128)
        line = pair_grad[:, strip * 128 : strip * 128 + 128]
        if shift:
            line = pltpu.roll(line, 128 - shift, 1)
        if shift + i > 128:
            more = pltpu.roll(pair_grad[:, strip * 128 + 128 : strip * 128 + 256], 128 - shift, 1)
            line = jnp.where(lane8 < 128 - shift, line, more)
        lower[:, i, :] = jnp.where(lane8 < i, line, 0.0)

    def back(q, carry):
        under = lower[q]
        both = (under[:, 0:PAD] + under.T[0:PAD, :]).astype(BF16)
        rows = rows_at(q * PAD, PAD, PAD)
        grad = mm(both, stack[rows, :]) * ROOT
        row = iota((PAD, WIDTH), 0)
        grad = jnp.where((row >= 1) & (row <= CAND), grad, 0.0).astype(BF16)
        cand_grad[rows, :] = grad
        ready, given = unit[rows, :], grad.astype(F32)
        along = jnp.mean(ready * given, axis=-1, keepdims=True)
        pre_grad[rows, :] = (wide(inv[rows, :], 4) * (given - ready * along)).astype(BF16)
        return carry

    lax.fori_loop(0, REQS, back, 0)

    def weight_term(tile, carry):
        cols = rows_at(tile * 256, 256, 256)
        term[cols, :] = tn(joined[:, cols], pre_grad[...])
        return carry

    lax.fori_loop(0, 4, weight_term, 0)

    rows, width = term.shape
    chunk = width // CHUNKS
    in_flight = {}

    def pass_on(c, number, src, dst, peer):
        in_flight[c, number] = send(src, dst, red_s.at[c, number], red_r.at[c, number], peer)

    def arrive(c, numbers):
        for number in numbers:
            in_flight[c, number].wait_recv()

    def step0(c):
        theirs = pl.multiple_of((1 - core) * (rows // 2), rows // 2)
        send0[c] = term[pl.ds(theirs, rows // 2), c * chunk : (c + 1) * chunk].astype(BF16)
        pass_on(c, 0, send0.at[c], recv0.at[c], other_core)

    def step1(c):
        arrive(c, [0])
        mine = pl.multiple_of(core * (rows // 2), rows // 2)
        total = term[pl.ds(mine, rows // 2), c * chunk : (c + 1) * chunk] + recv0[c].astype(F32)
        half[c] = total.reshape(N_X, rows // 8, chunk)
        send1[c] = total.astype(BF16).reshape(N_X, rows // 8, chunk)
        for k in range(1, N_X):
            to = lax.rem(x + k, N_X)
            pass_on(c, k, send1.at[c, to], recv1.at[c, k - 1], at_x(k))

    def step2(c):
        arrive(c, range(1, 4))
        total = half[c, x]
        for k in range(N_X - 1):
            total = total + recv1[c, k].astype(F32)
        half[c, 0] = total
        send2[c] = total.astype(BF16).reshape(N_Y, rows // 64, chunk)
        for k in range(1, N_Y):
            to = lax.rem(y + k, N_Y)
            pass_on(c, 3 + k, send2.at[c, to], recv2.at[c, k - 1], at_y(k))

    def step3(c):
        arrive(c, range(4, 11))
        total = half[c, 0, rows_at(y * (rows // 64), rows // 64, rows // 64)]
        for k in range(N_Y - 1):
            total = total + recv2[c, k].astype(F32)
        slots3[c, z] = total.astype(BF16)
        for k in range(1, N_Z):
            pass_on(c, 10 + k, slots3.at[c, z], slots3.at[c, z], at_z(k))

    def step4(c):
        arrive(c, range(11, 22))
        total = slots3[c, 0].astype(F32)
        for k in range(1, N_Z):
            total = total + slots3[c, k].astype(F32)
        fin4[c, y] = (total * (1.0 / (GROUP * N_X * N_Z))).astype(BF16)
        for k in range(1, N_Y):
            pass_on(c, 21 + k, fin4.at[c, y], fin4.at[c, y], at_y(k))

    def step5(c):
        arrive(c, range(22, 29))
        fin5[c, x] = fin4[c].reshape(rows // 8, chunk)
        for k in range(1, N_X):
            pass_on(c, 28 + k, fin5.at[c, x], fin5.at[c, x], at_x(k))

    def step6(c):
        arrive(c, range(29, 32))
        fin6[c, core] = fin5[c].reshape(rows // 2, chunk)
        pass_on(c, 32, fin6.at[c, core], fin6.at[c, core], other_core)

    def step7(c):
        arrive(c, [32])
        mean_out[:, c * chunk : (c + 1) * chunk] = fin6[c].reshape(rows, chunk)

    steps = (step0, step1, step2, step3, step4, step5, step6, step7)
    waves = [
        [(wave - c, c) for c in range(CHUNKS) if 0 <= wave - c < len(steps)]
        for wave in range(len(steps) + CHUNKS - 1)
    ]

    def run(wave):
        for step, c in waves[wave]:
            steps[step](c)

    run(0)

    def fill(four, carry):
        chosen = jnp.concatenate([place[four * 4 + j, 0:64, :] for j in range(4)], axis=0)
        picked = mm(chosen, cand_grad[...])
        for j in range(4):
            one = picked[j * 64 : j * 64 + CAP]
            both = jnp.concatenate([one[:, 0 : WIDTH // 2], one[:, WIDTH // 2 :]], axis=0)
            outbox[four * 4 + j] = both.astype(BF16)
        return carry

    lax.fori_loop(0, 4, fill, 0)
    my_box = inbox.at[rows_at(me * 2 * CAP, 2 * CAP, 16)]
    kept = pltpu.make_async_copy(outbox.at[me], my_box, w_sem.at[2])
    kept.start()
    run(1)
    box_got = []
    for k in range(1, GROUP):
        to = lax.rem(me + k, GROUP)
        box_got.append(send(outbox.at[to], my_box, box_s.at[k - 1], box_r.at[k - 1], at_shard(k)))

    shares = mm(own_mix[:, 0:NODES], feats[...]) + mm(own_mix[:, NODES:], halo[...])
    around = (shares * wide(1.0 / w_own_sum, 4)).astype(BF16)
    projected = mm(feats[...], gcn[0:WIDTH, :]) + mm(around, gcn[WIDTH:, :])
    root = lax.rsqrt(jnp.mean(projected * projected, axis=-1, keepdims=True) + 1e-06)
    emb_out[...] = (projected * root).astype(BF16)
    run(2)

    for copy in msg_got:
        copy.wait_recv()
    box_rows = GROUP * 2 * CAP
    lane16 = iota((16, 128), 1)
    marks = [jnp.zeros((16, 128), F32) for _ in range(box_rows // 128 + 1)]
    for p in range(GROUP):
        strip, shift = divmod(p * 2 * CAP, 128)
        line = jnp.where(lane16 < 2 * CAP, msg_in[p].astype(F32), 0.0)
        if shift:
            line = pltpu.roll(line, shift, 1)
        if shift + 2 * CAP > 128:
            marks[strip] = marks[strip] + jnp.where(lane16 >= shift, line, 0.0)
            marks[strip + 1] = marks[strip + 1] + jnp.where(lane16 < shift, line, 0.0)
        else:
            marks[strip] = marks[strip] + line
    run(3)
    for strip in range(box_rows // 128):
        line = lax.rem(iota((1, 128), 1) + strip * 128, 2 * CAP)
        goal = marks[strip][0:1, :]
        cols = slice(strip * 128, strip * 128 + 128)
        here = iota((NODES, 128), 0).astype(F32)
        spread[0:NODES, cols] = mark(here == jnp.where(line < CAP, goal, -1.0))
        spread[NODES:, cols] = mark(here == jnp.where(line < CAP, -1.0, goal))
    for wave in range(4, len(waves)):
        run(wave)

    for copy in box_got:
        copy.wait_recv()
    kept.wait()
    for part in range(2):
        cols = slice(part * NODES, part * NODES + NODES)
        grad_out[:, cols] = mm(spread[cols, :], inbox[...])
    for copy in sent:
        copy.wait_send()


def on_device(
    node_feats,
    send_rows,
    neighbors,
    neighbor_weight,
    gcn_weight,
    user_dense,
    cand_owner,
    cand_row,
    mlp_weight,
    out_weight,
    logit_grad,
):
    rows, width = gcn_weight.shape
    chunk = width // CHUNKS
    eighth, block = rows // 8, rows // 64
    vmem = pl.BlockSpec(memory_space=pltpu.VMEM)
    hbm = pl.BlockSpec(memory_space=pl.ANY)
    dma = pltpu.SemaphoreType.DMA
    embeddings, embed_grad, clicks, mean = pl.pallas_call(
        kernel,
        out_shape=(
            jax.ShapeDtypeStruct((NODES, WIDTH), BF16),
            jax.ShapeDtypeStruct((NODES, WIDTH), F32),
            jax.ShapeDtypeStruct((REQS, 128), F32),
            jax.ShapeDtypeStruct((rows, width), BF16),
        ),
        in_specs=[vmem, vmem, vmem, vmem, hbm, vmem, vmem, vmem, hbm, vmem, vmem],
        out_specs=(vmem, vmem, vmem, vmem),
        scratch_shapes=[
            pltpu.VMEM((GROUP, 144, 128), BF16),
            pltpu.VMEM((N_Y, 2 * NODES, WIDTH), BF16),
            pltpu.VMEM((SLOTS, 128), F32),
            pltpu.VMEM((SLOTS, 128), F32),
            pltpu.VMEM((GROUP, 128, SLOTS), BF16),
            pltpu.VMEM((GROUP, 16, 128), BF16),
            pltpu.VMEM((GROUP, 16, 128), BF16),
            pltpu.VMEM((SLOTS, 128), I16),
            pltpu.VMEM((DEG, SLOTS, 128), I16),
            pltpu.VMEM((DEG, SLOTS, 128), BF16),
            pltpu.VMEM((SLOTS, 128), F32),
            pltpu.VMEM((SLOTS, GROUP * BND), BF16),
            pltpu.VMEM((N_Y, 2 * SLOTS, 2 * NODES), BF16),
            pltpu.VMEM((GROUP * BND, 2 * NODES), BF16),
            pltpu.VMEM((GROUP * BND, WIDTH), BF16),
            pltpu.VMEM((DEG, NODES, 128), I16),
            pltpu.VMEM((DEG, NODES, 128), BF16),
            pltpu.VMEM((NODES, NODES + GROUP * BND), BF16),
            pltpu.VMEM((2 * SLOTS, WIDTH), F32),
            pltpu.VMEM((SLOTS, 2 * WIDTH), BF16),
            pltpu.VMEM((SLOTS, WIDTH), F32),
            pltpu.VMEM((SLOTS, 128), F32),
            pltpu.VMEM((SLOTS + PAD, WIDTH), BF16),
            pltpu.VMEM((REQS, PAD, 128), F32),
            pltpu.VMEM((REQS, PAD, 128), F32),
            pltpu.VMEM((REQS, PAIRS // 128 * 128 + 128), F32),
            pltpu.VMEM((SLOTS, WIDTH), BF16),
            pltpu.VMEM((SLOTS, WIDTH), BF16),
            pltpu.VMEM((rows, width), F32),
            pltpu.VMEM((GROUP, 2 * CAP, WIDTH // 2), BF16),
            pltpu.VMEM((GROUP * 2 * CAP, WIDTH // 2), BF16),
            pltpu.VMEM((2 * NODES, GROUP * 2 * CAP), BF16),
            pltpu.VMEM(mlp_weight.shape, BF16),
            pltpu.VMEM((rows, width), BF16),
            pltpu.VMEM((CHUNKS, rows // 2, chunk), BF16),
            pltpu.VMEM((CHUNKS, rows // 2, chunk), BF16),
            pltpu.VMEM((CHUNKS, N_X, eighth, chunk), F32),
            pltpu.VMEM((CHUNKS, N_X, eighth, chunk), BF16),
            pltpu.VMEM((CHUNKS, N_X - 1, eighth, chunk), BF16),
            pltpu.VMEM((CHUNKS, N_Y, block, chunk), BF16),
            pltpu.VMEM((CHUNKS, N_Y - 1, block, chunk), BF16),
            pltpu.VMEM((CHUNKS, N_Z, block, chunk), BF16),
            pltpu.VMEM((CHUNKS, N_Y, block, chunk), BF16),
            pltpu.VMEM((CHUNKS, N_X, eighth, chunk), BF16),
            pltpu.VMEM((CHUNKS, 2, rows // 2, chunk), BF16),
            dma((3,)),
            dma((8,)),
            dma((8,)),
            dma((8,)),
            dma((8,)),
            dma((16,)),
            dma((16,)),
            dma((16,)),
            dma((16,)),
            dma((GROUP - 1,)),
            dma((GROUP - 1,)),
            dma((GROUP - 1,)),
            dma((GROUP - 1,)),
            dma((CHUNKS, 33)),
            dma((CHUNKS, 33)),
        ],
        compiler_params=pltpu.CompilerParams(
            collective_id=0, has_side_effects=True, vmem_limit_bytes=58 * 1024 * 1024
        ),
    )(
        node_feats,
        send_rows,
        neighbors,
        neighbor_weight,
        gcn_weight,
        user_dense,
        cand_owner.reshape(REQS, CAND),
        cand_row,
        mlp_weight,
        out_weight.reshape(1, -1),
        logit_grad.reshape(REQS, 1),
    )
    return (embeddings, embed_grad, clicks[:, 0], mean.astype(F32))


def solution(mesh):
    return jax.shard_map(
        on_device,
        mesh=mesh,
        in_specs=(
            P(("shard", "rep"), None),
            P(("shard", "rep"), None, None),
            P(("shard", "rep"), None),
            P(("shard", "rep"), None),
            P(),
            P(("shard", "rep"), None),
            P(("shard", "rep"), None, None),
            P(("shard", "rep"), None),
            P(),
            P(),
            P(("shard", "rep")),
        ),
        out_specs=(P(("shard", "rep"), None), P(("shard", "rep"), None), P(("shard", "rep")), P()),
        check_vma=False,
    )
```

time: 663 us -> 154 us (0.23)
  waiting for transfers between devices: 546 us -> 0 us
  Pallas kernels: 0 us -> 141 us
  local copies, waits for them, and re-layouts: 49.5 us -> 9.36 us
  starting transfers between devices: 25.1 us -> 0 us
  other arithmetic: 18.5 us -> 2.83 us
  between operations: 14.5 us -> 0.65 us
  matrix products: 7.36 us -> 0 us
    psum x1 -> x0, waiting for transfers between devices: 477 us -> none  [on_device(): summed_grad = lax.psum(grad_term, ('shard', 'rep'))]
    pallas_call x0 -> x1, Pallas kernels: none -> 141 us  [on_device(): pl.pallas_call(kernel, out_shape=(jax.ShapeDtypeStruct((NODES, WIDTH), BF...]
    all_to_all x4 -> x0, waiting for transfers between devices: 69.1 us -> none  [the longest x1 24.4 us: on_device(): lax.all_to_all(looked_up, 'shard', split_axis=0, concat_axis=0, tiled=True)]
    gather x6 -> x0, local copies, waits for them, and re-layouts: 36 us -> none  [the longest x1 17.3 us: local_layer(): picked = tables[indices].astype(jnp.float32)]
    all_to_all x4 -> x0, starting transfers between devices: 25.1 us -> none  [the longest x1 13.8 us: on_device(): lax.all_to_all(wanted, 'shard', split_axis=0, concat_axis=0, tiled=True)]
    scatter-add x1 -> x0, other arithmetic: 7.26 us -> none  [on_device(): embed_grad = jnp.zeros((node_count, model_width), jnp.float32).at[asked.r...]
  transfers between devices with their start and end apart: 5 -> 0, of which waited for: 5 -> 0; matrix products, arithmetic and copies ran while one was open for 1% -> 0% of each run, Pallas kernels for 0% -> 0%
where the time goes in v2:
time: 154 us
  Pallas kernels  141 us (92%)
  local copies, waits for them, and re-layouts  9.36 us (6%)
  other arithmetic  2.83 us (2%)
    pallas_call x1, Pallas kernels, on_device(): pl.pallas_call(kernel, out_shape=(jax.ShapeDtypeStruct((NODES, WIDTH), BF...  141 us
    unnamed x6, local copies, waits for them, and re-layouts  5.41 us

profile of v2, /device:TPU:1, one launch (start us, length us, event | category | flops | bytes accessed | tf_op | source)
XLA Modules:
  0.0 154.0 jit_solution(17402804355558648909)
XLA Ops:
  0.6 1.3 reshape.18.out_weight
  1.9 1.3 copy.20.logit_grad
  3.2 1.5 copy.18.neighbors
  4.7 1.5 copy.19.weights
  6.2 141.1 %shard_map.138 = (bf16[256,512]{1,0:T(8,128)(2,1)}, f32[256,512]{1,0:T(8,128)}, f32[8,128]{1,0:T(8,128)}, bf16[1024,512]{1,0:T(8,128)(2,1)}) custom-call(bf16[256,512]{1,0:T(8,128)(2,1)} %feats.1, s32[1,16,32]{2,1,0:T(8,128)} %send_rows.1, s32[256,16]{1,0:T(8,128)} %copy.18.neighbors, f32[256,16]{1,0:T(8,128)} %copy.19.weights, bf16[1024,512]{1,0:T(8,128)(2,1)} %gcn_hbm.1, ...), custom_call_target="tpu_custom_call" | custom-call | tf_op jit(solution)/shard_map/pallas_call | solution.py:708
  147.3 0.0 copy-start
  147.3 1.4 slice_reduce_fusion
  148.7 2.8 %convert_element_type.3 = f32[1024,512]{1,0:T(8,128)} convert(bf16[1024,512]{1,0:T(8,128)(2,1)} %get-tuple-element.11) | non-fusion elementwise | flops 524288 | bytes 3145728 | tf_op jit(solution)/shard_map/convert_element_type | solution.py:796
  151.5 1.7 %copy.23 = bf16[256,512]{1,0:T(8,128)(2,1)} copy(bf16[256,512]{1,0:T(8,128)(2,1)} %get-tuple-element.16) | data formatting | bytes 524288
  153.2 0.0 copy-done
  153.2 0.8 copy.24
Async XLA Ops:
  147.3 5.9 %copy-start = (f32[256,512]{1,0:T(8,128)S(1)}, f32[256,512]{1,0:T(8,128)}, u32[]{:S(2)}) copy-start(f32[256,512]{1,0:T(8,128)} %get-tuple-element.17) | copy-start | bytes 1572868

commit v3 on v2

--- a/solution.py
+++ b/solution.py
@@ -8,11 +8,12 @@
 from jax.sharding import PartitionSpec as P
 
 MESH = pl.DeviceIdType.MESH
-F32, BF16, I32, I16 = jnp.float32, jnp.bfloat16, jnp.int32, jnp.int16
+F32, BF16, I32 = jnp.float32, jnp.bfloat16, jnp.int32
 N_X, N_Y, N_Z, GROUP = 4, 8, 12, 16
 NODES, WIDTH, DEG, BND = 256, 512, 16, 32
 REQS, CAND, PAD, CAP = 8, 50, 64, 56
 SLOTS = REQS * PAD
+LINES = SLOTS + NODES
 PAIRS = CAND * (CAND + 1) // 2
 CHUNKS = 2
 ROOT = 1.0 / math.sqrt(WIDTH)
@@ -62,24 +63,18 @@
     grad_out,
     click_out,
     mean_out,
+    lists,
     meta,
     table,
-    owner_b,
-    row_b,
     place,
     msg_out,
     msg_in,
-    cid,
-    gid,
-    wgt,
+    choose,
+    drawn,
+    held_by,
+    flat,
+    bound,
     wsum,
-    picks,
-    mix,
-    halo_pick,
-    halo,
-    own_id,
-    own_w,
-    own_mix,
     acc,
     joined,
     unit,
@@ -101,6 +96,7 @@
     half,
     send1,
     recv1,
+    tiled,
     send2,
     recv2,
     slots3,
@@ -172,21 +168,17 @@
         return copy
 
     ids = neighbors[...]
-    id_hi = lax.shift_right_logical(ids, 8).astype(F32).astype(BF16)
-    id_lo = jnp.bitwise_and(ids, 255).astype(F32).astype(BF16)
-    w_own = weights[...].astype(BF16)
-
-    def put(values, offset):
-        return mm(values, mark(iota((DEG, 128), 1) == iota((DEG, 128), 0) + offset))
-
-    packed = jnp.zeros((128, 128), F32)
+    lists[0:DEG, :] = lax.shift_right_logical(ids, 5).astype(F32)
+    lists[DEG : 2 * DEG, :] = jnp.bitwise_and(ids, BND - 1).astype(F32)
+    lists[2 * DEG : 3 * DEG, :] = weights[...]
+    lists[3 * DEG :, :] = jnp.zeros((DEG, NODES), F32)
+    sr = send_rows[0].astype(F32).astype(BF16)
+    sr = mm(sr, mark(jnp.bitwise_and(iota((BND, NODES), 1), BND - 1) == iota((BND, NODES), 0)))
     for part in range(2):
-        cut = slice(part * 128, part * 128 + 128)
-        base = part * 64
-        packed = packed + put(id_hi[cut], base) + put(id_lo[cut], base + 16) + put(w_own[cut], base + 32)
-    meta[me, 0:128, :] = packed.astype(BF16)
-    sr = send_rows[0].astype(F32).astype(BF16)
-    meta[me, 128:144, :] = mm(sr, mark(iota((BND, 128), 1) == iota((BND, 128), 0))).astype(BF16)
+        owner_of = lax.shift_right_logical(iota((GROUP, NODES), 1), 5) + part * 8
+        line = jnp.sum(jnp.where(iota((GROUP, NODES), 0) == owner_of, sr, 0.0), axis=0, keepdims=True)
+        lists[3 * DEG + part : 3 * DEG + part + 1, :] = line
+    meta[me] = lists[...].astype(BF16)
     table[y, rows_at(core * NODES, NODES, NODES), :] = feats[...]
 
     pl.semaphore_wait(barrier, len(peers))
@@ -273,9 +265,20 @@
 
     owner_col = jnp.where(valid, column(owners[...]), -1.0)
     row_col = jnp.where(valid, column(wanted[...]), 0.0)
-    owner_b[...] = owner_col
-    row_b[...] = row_col
-    cid[...] = jnp.where(valid, owner_col * NODES + row_col, -1.0).astype(I32).astype(I16)
+    owner16, row16 = owner_col.astype(BF16), row_col.astype(BF16)
+
+    ones16 = jnp.ones((SLOTS, 128), BF16)
+    zero16 = jnp.zeros((SLOTS, 128), BF16)
+    lane_lo = iota((SLOTS, 128), 1).astype(F32).astype(BF16)
+    lane_hi = (iota((SLOTS, 128), 1) + 128).astype(F32).astype(BF16)
+
+    def choose_self(p, carry):
+        here = jnp.where(owner16 == p.astype(F32).astype(BF16), row16, -ones16)
+        choose[p, 0:SLOTS, 0:128] = jnp.where(here == lane_lo, ones16, zero16)
+        choose[p, 0:SLOTS, 128:256] = jnp.where(here == lane_hi, ones16, zero16)
+        return carry
+
+    lax.fori_loop(0, GROUP, choose_self, 0)
 
     meta_step(0)
 
@@ -284,168 +287,135 @@
     below = mark(iota((SLOTS, SLOTS), 0) >= iota((SLOTS, SLOTS), 1))
     counts = mm(below, hits)
     rank = mm((jnp.where(owner_col == lanes, counts, 0.0)).astype(BF16), jnp.ones((128, 128), BF16))
-    slot_col = jnp.where(valid, owner_col * 128 + rank - 1.0, -4096.0)
-    slot_lane = slot_col.T[0:16, :]
+    rank_lane = jnp.broadcast_to((rank - 1.0).T[0:1, :], (64, SLOTS)).astype(BF16)
+    owner_lane = jnp.broadcast_to(owner_col.T[0:1, :], (64, SLOTS)).astype(BF16)
     row_lane = row_col.T[0:16, :].astype(BF16)
-
+    feat_step(0, 0)
     meta_step(1)
 
     def place_owner(owner, carry):
-        mine = slot_lane[0:1, :] - owner.astype(F32) * 128
-        at = iota((128, SLOTS), 0)
-        at = jnp.where(at >= CAP, at - CAP, at)
-        at = jnp.where(iota((128, SLOTS), 0) >= 2 * CAP, -30000, at)
-        chosen = mark(at.astype(F32) == mine)
-        place[owner] = chosen
-        msg_out[owner] = nt(row_lane, chosen).astype(BF16)
+        nobody = jnp.full((64, SLOTS), -1.0, BF16)
+        at = jnp.where(owner_lane == owner.astype(F32).astype(BF16), rank_lane, nobody)
+        goal = iota((64, SLOTS), 0).astype(F32).astype(BF16)
+        place[rows_at(owner * 64, 64, 64), :] = jnp.where(at == goal, nobody * nobody, nobody * 0)
         return carry
 
     lax.fori_loop(0, GROUP, place_owner, 0)
+    feat_step(0, 1)
     meta_step(2)
-    msg_in[me] = msg_out[me]
-    msg_got = []
-    for k in range(1, GROUP):
-        to = lax.rem(me + k, GROUP)
-        msg_got.append(send(msg_out.at[to], msg_in.at[me], msg_s.at[k - 1], msg_r.at[k - 1], at_shard(k)))
-    feat_step(0, 0)
-
-    w_own_sum = mm(w_own, jnp.ones((DEG, 128), BF16))
-
-    def own_k(k, carry):
-        pick = mark(iota((DEG, 128), 0) == k)
-        own_id[k] = (mm(id_hi, pick) * 256 + mm(id_lo, pick)).astype(I32).astype(I16)
-        own_w[k] = mm(w_own, pick).astype(BF16)
-        return carry
-
-    lax.fori_loop(0, DEG, own_k, 0)
-
-    def own_rows(tile, carry):
-        rows = rows_at(tile * 16, 16, 16)
-        found = [own_id[k, rows, :] for k in range(DEG)]
-        share = [own_w[k, rows, :] for k in range(DEG)]
-        for t in range(6):
-            lane = (iota((16, 128), 1) + t * 128).astype(I16)
-            total = jnp.zeros((16, 128), BF16)
-            for k in range(DEG):
-                total = total + jnp.where(found[k] == lane, share[k], jnp.zeros((16, 128), BF16))
-            own_mix[rows, t * 128 : t * 128 + 128] = total
-        return carry
-
-    lax.fori_loop(0, NODES // 16, own_rows, 0)
-
+    notes = nt(row_lane, place[...]).astype(BF16)
+    for two in range(GROUP // 2):
+        msg_out[two] = notes[:, two * 128 : two * 128 + 128]
+    msg_in[me] = msg_out[y]
+    feat_step(1, 0)
     meta_step(3)
     for d in core_order:
         metac_got[d].wait_recv()
-    feat_step(0, 1)
-
-    narrow = jnp.where(row_b[...] >= 128, row_b[...] - 128, row_b[...])
-    meta_id = jnp.where(valid, owner_b[...] * 128 + narrow, -1.0)
-
-    def meta_pick(p, total):
-        chosen = mark(meta_id == (iota((SLOTS, 128), 1) + p * 128).astype(F32))
-        return total + mm(chosen, meta[p, 0:128, :])
-
-    got = lax.fori_loop(0, GROUP, meta_pick, jnp.zeros((SLOTS, 128), F32))
-    got = jnp.where(row_b[...] >= 128, pltpu.roll(got, 64, 1), got)
-    lane128 = iota((SLOTS, 128), 1)
-    got = jnp.where(lane128 < 48, got, 0.0).astype(BF16)
-    wsum[...] = mm(got, mark(iota((128, 128), 0) >= 32))
-
-    owner16 = mark(owner_b[:, 0:GROUP] == iota((SLOTS, GROUP), 1).astype(F32))
-    mine16 = mark(iota((GROUP, 128), 0) == me)
-    for j in range(4):
-        tile = jnp.zeros((GROUP, 128), F32)
-        for i in range(4):
-            rows = meta[4 * j + i, 128:144, :].astype(F32)
-            tile = tile + (pltpu.roll(rows, 32 * i, 1) if i else rows)
-        tile = tile.astype(BF16)
-        picks[:, j * 128 : j * 128 + 128] = mm(owner16, tile).astype(BF16)
-        from_me = tn(tile, mine16)
-        odd = jnp.bitwise_and(lax.shift_right_logical(iota((128, 128), 0), 5), 1).astype(F32)
-        from_me = from_me + odd * NODES
-        for t in range(4):
-            lane = (iota((128, 128), 1) + t * 128).astype(F32)
-            halo_pick[j * 128 : j * 128 + 128, t * 128 : t * 128 + 128] = mark(from_me == lane)
-
-    def cand_k(k, carry):
-        spots = iota((128, 128), 0)
-        hi = mm(got, mark(spots == k))
-        lo = mm(got, mark(spots == k + 16))
-        wgt[k] = mm(got, mark(spots == k + 32)).astype(BF16)
-        ext = hi * 256 + lo - 256
-        ext16 = ext.astype(I32).astype(I16)
-        found = jnp.zeros((SLOTS, 128), BF16)
-        for j in range(4):
-            lane = (iota((SLOTS, 128), 1) + j * 128).astype(I16)
-            found = found + jnp.where(
-                ext16 == lane, picks[:, j * 128 : j * 128 + 128], jnp.zeros((SLOTS, 128), BF16)
-            )
-        far = mm(found, jnp.ones((128, 128), BF16))
-        source = jnp.floor(ext * (1.0 / BND))
-        where = jnp.where(hi < 0.5, owner_b[...] * NODES + lo, source * NODES + far)
-        gid[k] = where.astype(I32).astype(I16)
+
+    def list_of(p, total):
+        return total + nt(choose[p, 0:SLOTS, :], meta[p, 0 : 3 * DEG, :])
+
+    got = lax.fori_loop(0, GROUP, list_of, jnp.zeros((SLOTS, 3 * DEG), F32))
+    own = nt(mark(iota((NODES, NODES), 0) == iota((NODES, NODES), 1)), meta[me, 0 : 3 * DEG, :])
+    drawn[:, 3 * DEG :] = jnp.zeros((LINES, 128 - 3 * DEG), F32)
+    drawn[:, 0 : 3 * DEG] = jnp.concatenate([got, own], axis=0)
+    held_by[0:SLOTS, :] = owner_col
+    held_by[SLOTS:, :] = jnp.zeros((NODES, 128), F32) + me.astype(F32)
+    got = drawn[:, 0 : 3 * DEG].astype(BF16)
+    wsum[...] = mm(got, mark(iota((3 * DEG, 128), 0) >= 2 * DEG))
+    batches = LINES // 16
+    group_of = lax.shift_right_logical(iota((batches, 128), 1), 4)
+    laid = [[jnp.zeros((batches, 128), F32) for _ in range(2)] for _ in range(4)]
+    for c in range(16):
+        here = group_of == c % 8
+        every = pl.ds(c, batches, stride=16)
+        lines = drawn[every, :]
+        for field in range(3):
+            turn = (c - field) * DEG % 128
+            line = pltpu.roll(lines, turn, 1) if turn else lines
+            laid[field][c // 8] = jnp.where(here, line, laid[field][c // 8])
+        laid[3][c // 8] = jnp.where(here, held_by[every, :], laid[3][c // 8])
+    part_of, rest, share, keeper = [jnp.concatenate(halves, axis=1) for halves in laid]
+    inside = part_of < NODES // BND
+    source = jnp.where(inside, keeper, part_of - NODES // BND)
+    which = keeper * BND + rest
+    member_at = lax.shift_right_logical(iota((batches, 256), 1), 4).astype(F32)
+    for number, values in enumerate((
+        source * 16 + member_at,
+        jnp.where(inside, part_of * BND + rest, -1.0),
+        share,
+        jnp.where(inside | (which >= 256), -1.0, which),
+        jnp.where(inside | (which < 256), -1.0, which - 256),
+        source,
+    )):
+        flat[:, number * 256 : number * 256 + 256] = values
+    all_bounds = meta[:, 3 * DEG : 4 * DEG, :].reshape(GROUP * 16, NODES)
+    for part in range(2):
+        pick = mark(iota((GROUP, GROUP * 16), 1) == iota((GROUP, GROUP * 16), 0) * 16 + part)
+        bound[part] = mm(pick, all_bounds).astype(BF16)
+    feat_step(1, 1)
+
+    def build_one(batch):
+        one, nothing = jnp.ones((16, 256), BF16), jnp.zeros((16, 256), BF16)
+
+        def line(field):
+            return flat[pl.ds(batch, 1), field * 256 : field * 256 + 256]
+
+        def tall(values):
+            return jnp.broadcast_to(values, (16, 256)).astype(BF16)
+
+        def chart(values, entry):
+            strips = []
+            for i in range(16):
+                goal = (iota((16, 256), 0) + i * 16).astype(F32).astype(BF16)
+                strips.append(jnp.where(values == goal, entry, nothing))
+            return jnp.concatenate(strips, axis=0)
+
+        far = mm(bound[0], chart(tall(line(3)), one)) + mm(bound[1], chart(tall(line(4)), one))
+        far = jnp.where(iota((GROUP, 256), 0).astype(F32) == line(5), far, 0.0)
+        near = line(1)
+        low = jnp.where(near < 0, jnp.sum(far, axis=0, keepdims=True), near)
+        mixed = nt(chart(tall(line(0)), tall(line(2))), chart(tall(low), one)).astype(BF16)
+        choose[:, rows_at(SLOTS + batch * 16, 16, 16), :] = mixed.reshape(GROUP, 16, 256)
+
+    def build(pair, carry):
+        build_one(pair * 2)
+        build_one(pair * 2 + 1)
         return carry
 
-    lax.fori_loop(0, DEG, cand_k, 0)
-    feat_step(1, 0)
-
-    def build(d):
-        block = chip(d)
-
-        def rows_of(tile, carry):
-            rows = rows_at(tile * 16, 16, 16)
-            found = [gid[k, rows, :] for k in range(DEG)]
-            share = [wgt[k, rows, :] for k in range(DEG)]
-            itself = cid[rows, :]
-            nothing = jnp.zeros((16, 128), BF16)
-            for t in range(4):
-                lane = (iota((16, 128), 1) + (block * 512 + t * 128)).astype(I16)
-                cols = slice(t * 128, t * 128 + 128)
-                total = nothing
-                for k in range(DEG):
-                    total = total + jnp.where(found[k] == lane, share[k], nothing)
-                mix[block, rows, cols] = jnp.where(itself == lane, jnp.ones((16, 128), BF16), nothing)
-                mix[block, rows_at(SLOTS + tile * 16, 16, 16), cols] = total
-            return carry
-
-        lax.fori_loop(0, SLOTS // 16, rows_of, 0)
-
-    def absorb(d, first=False):
-        block = chip(d)
-        for part in range(2):
-            featc_got[d, part].wait_recv()
+    def absorb(chips, first=False):
+        blocks = [chip(d) for d in chips]
+        for d in chips:
+            for part in range(2):
+                featc_got[d, part].wait_recv()
 
         def rows_of(tile, carry):
             rows = rows_at(tile * 256, 256, 256)
-            product = mm(mix[block, rows, :], table[block])
-            acc[rows, :] = product if first else acc[rows, :] + product
+            product = None if first else acc[rows, :]
+            for block in blocks:
+                for i in range(2):
+                    more = mm(choose[block * 2 + i, rows, :], table[block, i * NODES : (i + 1) * NODES, :])
+                    product = more if product is None else product + more
+            acc[rows, :] = product
             return carry
 
         lax.fori_loop(0, 2 * SLOTS // 256, rows_of, 0)
-        pick = rows_at(block * 64, 64, 64)
-        halo[pick, :] = mm(halo_pick[pick, :], table[block]).astype(BF16)
-
-    build(0)
-    absorb(0, True)
-    feat_step(1, 1)
-    build(-1)
-    absorb(-1)
-    build(1)
-    absorb(1)
+
+    lax.fori_loop(0, 8, build, 0)
     feat_step(2, 0)
-    build(-2)
-    build(2)
+    lax.fori_loop(8, SLOTS // 32, build, 0)
+    absorb((0,), True)
     feat_step(2, 1)
-    absorb(-2)
-    absorb(2)
-    build(-3)
-    build(3)
-    build(4)
+    absorb((-1, 1))
+    absorb((-2, 2))
     feat_step(3, 0)
     feat_step(3, 1)
-    absorb(-3)
-    absorb(3)
-    absorb(4)
+    absorb((-3, 3))
+    absorb((4,))
+    msg_got = []
+    for k in range(1, GROUP):
+        to = lax.div(lax.rem(me + k, GROUP), 2)
+        msg_got.append(send(msg_out.at[to], msg_in.at[me], msg_s.at[k - 1], msg_r.at[k - 1], at_shard(k)))
 
     local[0].wait()
 
@@ -499,12 +469,14 @@
     pre = pre + mm(tail, mlp[split : WIDTH + PAIRS, :])
     bend = math.sqrt(2.0 / math.pi)
     curve = jnp.tanh(bend * (pre + 0.044715 * (pre * pre * pre)))
-    hidden = (pre * (0.5 * (1.0 + curve))).astype(BF16).astype(F32)
-    out_w = out_weight[...].astype(F32)
-    click = jnp.sum(hidden * out_w, axis=1, keepdims=True)
-    click_out[...] = jnp.broadcast_to(click, (REQS, 128))
+    hidden = (pre * (0.5 * (1.0 + curve))).astype(BF16)
+    out_w = out_weight[...].astype(F32).reshape(1, -1)
+    click_out[...] = nt(jnp.broadcast_to(out_w, (REQS, out_w.shape[1])).astype(BF16), hidden)[0]
+    given_logit = jnp.zeros((REQS, 1), F32)
+    for q in range(REQS):
+        given_logit = jnp.where(iota((REQS, 1), 0) == q, logit_grad[q], given_logit)
     slope = 0.5 * (1.0 + curve) + 0.5 * pre * (1.0 - curve * curve) * bend * (1.0 + 3 * 0.044715 * pre * pre)
-    hidden_grad = (logit_grad[...] * out_w * slope).astype(BF16)
+    hidden_grad = (given_logit * out_w * slope).astype(BF16)
     pair_grad[:, whole:] = jnp.zeros((REQS, 128), F32)
     pair_grad[:, 0:whole] = nt(hidden_grad, mlp[WIDTH:split, :])
     pair_grad[:, whole:PAIRS] = nt(hidden_grad, mlp[split : WIDTH + PAIRS, :])
@@ -535,6 +507,27 @@
 
     lax.fori_loop(0, REQS, back, 0)
 
+    def fill(four, carry):
+        picked = mm(place[rows_at(four * 256, 256, 256), :], cand_grad[...])
+        for j in range(4):
+            one = picked[j * 64 : j * 64 + CAP]
+            both = jnp.concatenate([one[:, 0 : WIDTH // 2], one[:, WIDTH // 2 :]], axis=0)
+            outbox[four * 4 + j] = both.astype(BF16)
+        return carry
+
+    lax.fori_loop(0, 4, fill, 0)
+    my_box = inbox.at[rows_at(me * 2 * CAP, 2 * CAP, 16)]
+    box_got = []
+
+    def send_boxes(steps_away):
+        for k in steps_away:
+            to = lax.rem(me + k, GROUP)
+            box_got.append(send(outbox.at[to], my_box, box_s.at[k - 1], box_r.at[k - 1], at_shard(k)))
+
+    send_boxes((8, 7, 9, 6, 10, 1, 15, 2, 14, 3, 13))
+    kept = pltpu.make_async_copy(outbox.at[me], my_box, w_sem.at[2])
+    kept.start()
+
     def weight_term(tile, carry):
         cols = rows_at(tile * 256, 256, 256)
         term[cols, :] = tn(joined[:, cols], pre_grad[...])
@@ -573,44 +566,50 @@
         total = half[c, x]
         for k in range(N_X - 1):
             total = total + recv1[c, k].astype(F32)
-        half[c, 0] = total
-        send2[c] = total.astype(BF16).reshape(N_Y, rows // 64, chunk)
+        for j in range(chunk // 128):
+            tiles = total[:, j * 128 : j * 128 + 128].reshape(8, 16, 128)
+            tiled[c, j * 8 : j * 8 + 8] = tiles
+            send2[c, j * 8 : j * 8 + 8] = tiles.astype(BF16)
+        tiled[c, 16:24] = jnp.zeros((8, 16, 128), F32)
+        send2[c, 16:24] = jnp.zeros((8, 16, 128), BF16)
+        for k in range(1, N_Z):
+            to = lax.rem(z + k, N_Z)
+            pass_on(c, 3 + k, send2.at[c, pl.ds(to * 2, 2)], recv2.at[c, k - 1], at_z(k))
+
+    def step3(c):
+        arrive(c, range(4, 15))
+        total = tiled[c, pl.ds(z * 2, 2)]
+        for k in range(N_Z - 1):
+            total = total + recv2[c, k].astype(F32)
+        slots3[c, y] = total.astype(BF16)
         for k in range(1, N_Y):
-            to = lax.rem(y + k, N_Y)
-            pass_on(c, 3 + k, send2.at[c, to], recv2.at[c, k - 1], at_y(k))
-
-    def step3(c):
-        arrive(c, range(4, 11))
-        total = half[c, 0, rows_at(y * (rows // 64), rows // 64, rows // 64)]
-        for k in range(N_Y - 1):
-            total = total + recv2[c, k].astype(F32)
-        slots3[c, z] = total.astype(BF16)
+            pass_on(c, 14 + k, slots3.at[c, y], slots3.at[c, y], at_y(k))
+
+    def step4(c):
+        arrive(c, range(15, 22))
+        total = slots3[c, 0].astype(F32)
+        for k in range(1, N_Y):
+            total = total + slots3[c, k].astype(F32)
+        fin4[c, z] = (total * (1.0 / (GROUP * N_X * N_Z))).astype(BF16)
         for k in range(1, N_Z):
-            pass_on(c, 10 + k, slots3.at[c, z], slots3.at[c, z], at_z(k))
-
-    def step4(c):
-        arrive(c, range(11, 22))
-        total = slots3[c, 0].astype(F32)
-        for k in range(1, N_Z):
-            total = total + slots3[c, k].astype(F32)
-        fin4[c, y] = (total * (1.0 / (GROUP * N_X * N_Z))).astype(BF16)
-        for k in range(1, N_Y):
-            pass_on(c, 21 + k, fin4.at[c, y], fin4.at[c, y], at_y(k))
+            pass_on(c, 21 + k, fin4.at[c, z], fin4.at[c, z], at_z(k))
 
     def step5(c):
-        arrive(c, range(22, 29))
-        fin5[c, x] = fin4[c].reshape(rows // 8, chunk)
+        arrive(c, range(22, 33))
+        fin5[c, x] = fin4[c].reshape(24, 16, 128)[0:16]
         for k in range(1, N_X):
-            pass_on(c, 28 + k, fin5.at[c, x], fin5.at[c, x], at_x(k))
+            pass_on(c, 32 + k, fin5.at[c, x], fin5.at[c, x], at_x(k))
 
     def step6(c):
-        arrive(c, range(29, 32))
-        fin6[c, core] = fin5[c].reshape(rows // 2, chunk)
-        pass_on(c, 32, fin6.at[c, core], fin6.at[c, core], other_core)
+        arrive(c, range(33, 36))
+        fin6[c, core] = fin5[c]
+        pass_on(c, 36, fin6.at[c, core], fin6.at[c, core], other_core)
 
     def step7(c):
-        arrive(c, [32])
-        mean_out[:, c * chunk : (c + 1) * chunk] = fin6[c].reshape(rows, chunk)
+        arrive(c, [36])
+        for j in range(chunk // 128):
+            done = fin6[c, :, :, j * 8 : j * 8 + 8].reshape(rows, 128)
+            mean_out[:, c * chunk + j * 128 : c * chunk + j * 128 + 128] = done
 
     steps = (step0, step1, step2, step3, step4, step5, step6, step7)
     waves = [
@@ -623,32 +622,20 @@
             steps[step](c)
 
     run(0)
-
-    def fill(four, carry):
-        chosen = jnp.concatenate([place[four * 4 + j, 0:64, :] for j in range(4)], axis=0)
-        picked = mm(chosen, cand_grad[...])
-        for j in range(4):
-            one = picked[j * 64 : j * 64 + CAP]
-            both = jnp.concatenate([one[:, 0 : WIDTH // 2], one[:, WIDTH // 2 :]], axis=0)
-            outbox[four * 4 + j] = both.astype(BF16)
-        return carry
-
-    lax.fori_loop(0, 4, fill, 0)
-    my_box = inbox.at[rows_at(me * 2 * CAP, 2 * CAP, 16)]
-    kept = pltpu.make_async_copy(outbox.at[me], my_box, w_sem.at[2])
-    kept.start()
     run(1)
-    box_got = []
-    for k in range(1, GROUP):
-        to = lax.rem(me + k, GROUP)
-        box_got.append(send(outbox.at[to], my_box, box_s.at[k - 1], box_r.at[k - 1], at_shard(k)))
-
-    shares = mm(own_mix[:, 0:NODES], feats[...]) + mm(own_mix[:, NODES:], halo[...])
-    around = (shares * wide(1.0 / w_own_sum, 4)).astype(BF16)
+    lax.fori_loop(SLOTS // 32, LINES // 32, build, 0)
+    run(2)
+
+    def own_part(p, total):
+        block = table[lax.div(p, 2), rows_at(lax.rem(p, 2) * NODES, NODES, NODES), :]
+        return total + mm(choose[p, 2 * SLOTS :, :], block)
+
+    shares = lax.fori_loop(0, GROUP, own_part, jnp.zeros((NODES, WIDTH), F32))
+    around = (shares * wide(1.0 / wsum[SLOTS:, :], 4)).astype(BF16)
     projected = mm(feats[...], gcn[0:WIDTH, :]) + mm(around, gcn[WIDTH:, :])
     root = lax.rsqrt(jnp.mean(projected * projected, axis=-1, keepdims=True) + 1e-06)
     emb_out[...] = (projected * root).astype(BF16)
-    run(2)
+    run(3)
 
     for copy in msg_got:
         copy.wait_recv()
@@ -657,7 +644,10 @@
     marks = [jnp.zeros((16, 128), F32) for _ in range(box_rows // 128 + 1)]
     for p in range(GROUP):
         strip, shift = divmod(p * 2 * CAP, 128)
-        line = jnp.where(lane16 < 2 * CAP, msg_in[p].astype(F32), 0.0)
+        line = msg_in[p].astype(F32)
+        line = jnp.where(core == 1, pltpu.roll(line, 64, 1), line)
+        line = jnp.where(lane16 < CAP, line, 0.0)
+        line = line + pltpu.roll(line, CAP, 1)
         if shift:
             line = pltpu.roll(line, shift, 1)
         if shift + 2 * CAP > 128:
@@ -665,7 +655,8 @@
             marks[strip + 1] = marks[strip + 1] + jnp.where(lane16 < shift, line, 0.0)
         else:
             marks[strip] = marks[strip] + line
-    run(3)
+    run(4)
+    send_boxes((4, 12, 5, 11))
     for strip in range(box_rows // 128):
         line = lax.rem(iota((1, 128), 1) + strip * 128, 2 * CAP)
         goal = marks[strip][0:1, :]
@@ -673,7 +664,7 @@
         here = iota((NODES, 128), 0).astype(F32)
         spread[0:NODES, cols] = mark(here == jnp.where(line < CAP, goal, -1.0))
         spread[NODES:, cols] = mark(here == jnp.where(line < CAP, -1.0, goal))
-    for wave in range(4, len(waves)):
+    for wave in range(5, len(waves)):
         run(wave)
 
     for copy in box_got:
@@ -701,39 +692,34 @@
 ):
     rows, width = gcn_weight.shape
     chunk = width // CHUNKS
-    eighth, block = rows // 8, rows // 64
+    eighth = rows // 8
     vmem = pl.BlockSpec(memory_space=pltpu.VMEM)
     hbm = pl.BlockSpec(memory_space=pl.ANY)
+    smem = pl.BlockSpec(memory_space=pltpu.SMEM)
     dma = pltpu.SemaphoreType.DMA
     embeddings, embed_grad, clicks, mean = pl.pallas_call(
         kernel,
         out_shape=(
             jax.ShapeDtypeStruct((NODES, WIDTH), BF16),
             jax.ShapeDtypeStruct((NODES, WIDTH), F32),
-            jax.ShapeDtypeStruct((REQS, 128), F32),
+            jax.ShapeDtypeStruct((REQS,), F32),
             jax.ShapeDtypeStruct((rows, width), BF16),
         ),
-        in_specs=[vmem, vmem, vmem, vmem, hbm, vmem, vmem, vmem, hbm, vmem, vmem],
+        in_specs=[vmem, vmem, vmem, vmem, hbm, vmem, vmem, vmem, hbm, vmem, smem],
         out_specs=(vmem, vmem, vmem, vmem),
         scratch_shapes=[
-            pltpu.VMEM((GROUP, 144, 128), BF16),
+            pltpu.VMEM((4 * DEG, NODES), F32),
+            pltpu.VMEM((GROUP, 4 * DEG, NODES), BF16),
             pltpu.VMEM((N_Y, 2 * NODES, WIDTH), BF16),
-            pltpu.VMEM((SLOTS, 128), F32),
-            pltpu.VMEM((SLOTS, 128), F32),
-            pltpu.VMEM((GROUP, 128, SLOTS), BF16),
+            pltpu.VMEM((GROUP * 64, SLOTS), BF16),
+            pltpu.VMEM((GROUP // 2, 16, 128), BF16),
             pltpu.VMEM((GROUP, 16, 128), BF16),
-            pltpu.VMEM((GROUP, 16, 128), BF16),
-            pltpu.VMEM((SLOTS, 128), I16),
-            pltpu.VMEM((DEG, SLOTS, 128), I16),
-            pltpu.VMEM((DEG, SLOTS, 128), BF16),
-            pltpu.VMEM((SLOTS, 128), F32),
-            pltpu.VMEM((SLOTS, GROUP * BND), BF16),
-            pltpu.VMEM((N_Y, 2 * SLOTS, 2 * NODES), BF16),
-            pltpu.VMEM((GROUP * BND, 2 * NODES), BF16),
-            pltpu.VMEM((GROUP * BND, WIDTH), BF16),
-            pltpu.VMEM((DEG, NODES, 128), I16),
-            pltpu.VMEM((DEG, NODES, 128), BF16),
-            pltpu.VMEM((NODES, NODES + GROUP * BND), BF16),
+            pltpu.VMEM((GROUP, SLOTS + LINES, NODES), BF16),
+            pltpu.VMEM((LINES, 128), F32),
+            pltpu.VMEM((LINES, 128), F32),
+            pltpu.VMEM((LINES // 16, 6 * 256), F32),
+            pltpu.VMEM((2, GROUP, NODES), BF16),
+            pltpu.VMEM((LINES, 128), F32),
             pltpu.VMEM((2 * SLOTS, WIDTH), F32),
             pltpu.VMEM((SLOTS, 2 * WIDTH), BF16),
             pltpu.VMEM((SLOTS, WIDTH), F32),
@@ -755,12 +741,13 @@
             pltpu.VMEM((CHUNKS, N_X, eighth, chunk), F32),
             pltpu.VMEM((CHUNKS, N_X, eighth, chunk), BF16),
             pltpu.VMEM((CHUNKS, N_X - 1, eighth, chunk), BF16),
-            pltpu.VMEM((CHUNKS, N_Y, block, chunk), BF16),
-            pltpu.VMEM((CHUNKS, N_Y - 1, block, chunk), BF16),
-            pltpu.VMEM((CHUNKS, N_Z, block, chunk), BF16),
-            pltpu.VMEM((CHUNKS, N_Y, block, chunk), BF16),
-            pltpu.VMEM((CHUNKS, N_X, eighth, chunk), BF16),
-            pltpu.VMEM((CHUNKS, 2, rows // 2, chunk), BF16),
+            pltpu.VMEM((CHUNKS, 24, 16, 128), F32),
+            pltpu.VMEM((CHUNKS, 24, 16, 128), BF16),
+            pltpu.VMEM((CHUNKS, N_Z - 1, 2, 16, 128), BF16),
+            pltpu.VMEM((CHUNKS, N_Y, 2, 16, 128), BF16),
+            pltpu.VMEM((CHUNKS, N_Z, 2, 16, 128), BF16),
+            pltpu.VMEM((CHUNKS, N_X, 16, 16, 128), BF16),
+            pltpu.VMEM((CHUNKS, 2, N_X, 16, 16, 128), BF16),
             dma((3,)),
             dma((8,)),
             dma((8,)),
@@ -774,8 +761,8 @@
             dma((GROUP - 1,)),
             dma((GROUP - 1,)),
             dma((GROUP - 1,)),
-            dma((CHUNKS, 33)),
-            dma((CHUNKS, 33)),
+            dma((CHUNKS, 37)),
+            dma((CHUNKS, 37)),
         ],
         compiler_params=pltpu.CompilerParams(
             collective_id=0, has_side_effects=True, vmem_limit_bytes=58 * 1024 * 1024
@@ -783,17 +770,17 @@
     )(
         node_feats,
         send_rows,
-        neighbors,
-        neighbor_weight,
+        neighbors.T,
+        neighbor_weight.T,
         gcn_weight,
         user_dense,
         cand_owner.reshape(REQS, CAND),
         cand_row,
         mlp_weight,
-        out_weight.reshape(1, -1),
-        logit_grad.reshape(REQS, 1),
+        out_weight,
+        logit_grad,
     )
-    return (embeddings, embed_grad, clicks[:, 0], mean.astype(F32))
+    return (embeddings, embed_grad, clicks, mean.astype(F32))
 
 
 def solution(mesh):

time: 154 us -> 120 us (0.78)
  Pallas kernels: 141 us -> 114 us
  local copies, waits for them, and re-layouts: 9.36 us -> 2.98 us
    pallas_call x1, Pallas kernels: 141 us -> 114 us  [on_device(): pl.pallas_call(kernel, out_shape=(jax.ShapeDtypeStruct((NODES, WIDTH), BF...]
    reshape x2 -> x0, local copies, waits for them, and re-layouts: 2.6 us -> none  [the longest x1 1.32 us: on_device(): logit_grad.reshape(REQS, 1)]
    unnamed x6 -> x7, local copies, waits for them, and re-layouts: 5.41 us -> 2.98 us
where the time goes in v3:
time: 120 us
  Pallas kernels  114 us (95%)
  local copies, waits for them, and re-layouts  2.98 us (2%)
  other arithmetic  2.89 us (2%)
    pallas_call x1, Pallas kernels, on_device(): pl.pallas_call(kernel, out_shape=(jax.ShapeDtypeStruct((NODES, WIDTH), BF...  114 us
    unnamed x7, local copies, waits for them, and re-layouts  2.98 us
    convert_element_type x1, other arithmetic, on_device(): return (embeddings, embed_grad, clicks, mean.astype(F32))  2.89 us

profile of v3, /device:TPU:1, one launch (start us, length us, event | category | flops | bytes accessed | tf_op | source)
XLA Modules:
  0.0 120.1 jit_solution(14196925937496696729)
XLA Ops:
  0.6 113.5 %shard_map.138 = (bf16[256,512]{1,0:T(8,128)(2,1)}, f32[256,512]{1,0:T(8,128)}, f32[8]{0:T(128)}, bf16[1024,512]{1,0:T(8,128)(2,1)}) custom-call(bf16[256,512]{1,0:T(8,128)(2,1)} %feats.1, s32[1,16,32]{2,1,0:T(8,128)} %send_rows.1, s32[16,256]{1,0:T(8,128)} %bitcast.3, f32[16,256]{1,0:T(8,128)} %bitcast.4, bf16[1024,512]{1,0:T(8,128)(2,1)} %gcn_hbm.1, ...), custom_call_target="tpu_custom_call" | custom-call | tf_op jit(solution)/shard_map/pallas_call | solution.py:700
  114.2 0.0 copy-start
  114.2 0.0 copy-start.1
  114.2 2.9 %convert_element_type.3 = f32[1024,512]{1,0:T(8,128)} convert(bf16[1024,512]{1,0:T(8,128)(2,1)} %get-tuple-element.11) | non-fusion elementwise | flops 524288 | bytes 3145728 | tf_op jit(solution)/shard_map/convert_element_type | solution.py:783
  117.1 1.7 %copy.18 = bf16[256,512]{1,0:T(8,128)(2,1)} copy(bf16[256,512]{1,0:T(8,128)(2,1)} %get-tuple-element.16) | data formatting | bytes 524288
  118.7 0.0 copy-done
  118.7 0.8 copy.19
  119.5 0.0 copy-done.1
  119.5 0.5 copy.20
Async XLA Ops:
  114.2 4.6 %copy-start = (f32[256,512]{1,0:T(8,128)S(1)}, f32[256,512]{1,0:T(8,128)}, u32[]{:S(2)}) copy-start(f32[256,512]{1,0:T(8,128)} %get-tuple-element.17) | copy-start | bytes 1572868
  114.2 5.4 %copy-start.1 = (f32[8]{0:T(128)S(1)}, f32[8]{0:T(128)}, u32[]{:S(2)}) copy-start(f32[8]{0:T(128)} %get-tuple-element.18) | copy-start | bytes 100

commit v4 on v3

--- a/solution.py
+++ b/solution.py
@@ -312,11 +312,15 @@
     for d in core_order:
         metac_got[d].wait_recv()
 
-    def list_of(p, total):
-        return total + nt(choose[p, 0:SLOTS, :], meta[p, 0 : 3 * DEG, :])
-
-    got = lax.fori_loop(0, GROUP, list_of, jnp.zeros((SLOTS, 3 * DEG), F32))
+    def list_of(four, total):
+        for i in range(4):
+            p = four * 4 + i
+            total = total + nt(choose[p, 0:SLOTS, :], meta[p, 0 : 3 * DEG, :])
+        return total
+
+    got = lax.fori_loop(0, GROUP // 4, list_of, jnp.zeros((SLOTS, 3 * DEG), F32))
     own = nt(mark(iota((NODES, NODES), 0) == iota((NODES, NODES), 1)), meta[me, 0 : 3 * DEG, :])
+    feat_step(1, 1)
     drawn[:, 3 * DEG :] = jnp.zeros((LINES, 128 - 3 * DEG), F32)
     drawn[:, 0 : 3 * DEG] = jnp.concatenate([got, own], axis=0)
     held_by[0:SLOTS, :] = owner_col
@@ -353,7 +357,6 @@
     for part in range(2):
         pick = mark(iota((GROUP, GROUP * 16), 1) == iota((GROUP, GROUP * 16), 0) * 16 + part)
         bound[part] = mm(pick, all_bounds).astype(BF16)
-    feat_step(1, 1)
 
     def build_one(batch):
         one, nothing = jnp.ones((16, 256), BF16), jnp.zeros((16, 256), BF16)
@@ -404,18 +407,18 @@
     lax.fori_loop(0, 8, build, 0)
     feat_step(2, 0)
     lax.fori_loop(8, SLOTS // 32, build, 0)
+    feat_step(2, 1)
+    msg_got = []
+    for k in range(1, GROUP):
+        to = lax.div(lax.rem(me + k, GROUP), 2)
+        msg_got.append(send(msg_out.at[to], msg_in.at[me], msg_s.at[k - 1], msg_r.at[k - 1], at_shard(k)))
     absorb((0,), True)
-    feat_step(2, 1)
     absorb((-1, 1))
     absorb((-2, 2))
     feat_step(3, 0)
     feat_step(3, 1)
     absorb((-3, 3))
     absorb((4,))
-    msg_got = []
-    for k in range(1, GROUP):
-        to = lax.div(lax.rem(me + k, GROUP), 2)
-        msg_got.append(send(msg_out.at[to], msg_in.at[me], msg_s.at[k - 1], msg_r.at[k - 1], at_shard(k)))
 
     local[0].wait()
 
@@ -441,11 +444,11 @@
     lax.fori_loop(0, SLOTS // 256, embed, 0)
     stack[SLOTS : SLOTS + PAD, :] = jnp.zeros((PAD, WIDTH), BF16)
 
-    def gram(q, carry):
+    def gram_one(q):
         grams[q] = nt(stack[rows_at(q * PAD, PAD, PAD), :], stack[rows_at(q * PAD, 2 * PAD, PAD), :]) * ROOT
-        return carry
-
-    lax.fori_loop(0, REQS, gram, 0)
+
+    for q in range(REQS):
+        gram_one(q)
 
     lane8 = iota((REQS, 128), 1)
     strips = [jnp.zeros((REQS, 128), F32) for _ in range(PAIRS // 128 + 2)]
@@ -492,7 +495,7 @@
             line = jnp.where(lane8 < 128 - shift, line, more)
         lower[:, i, :] = jnp.where(lane8 < i, line, 0.0)
 
-    def back(q, carry):
+    def back_one(q):
         under = lower[q]
         both = (under[:, 0:PAD] + under.T[0:PAD, :]).astype(BF16)
         rows = rows_at(q * PAD, PAD, PAD)
@@ -503,9 +506,13 @@
         ready, given = unit[rows, :], grad.astype(F32)
         along = jnp.mean(ready * given, axis=-1, keepdims=True)
         pre_grad[rows, :] = (wide(inv[rows, :], 4) * (given - ready * along)).astype(BF16)
+
+    def back(four, carry):
+        for q in range(4):
+            back_one(four * 4 + q)
         return carry
 
-    lax.fori_loop(0, REQS, back, 0)
+    lax.fori_loop(0, REQS // 4, back, 0)
 
     def fill(four, carry):
         picked = mm(place[rows_at(four * 256, 256, 256), :], cand_grad[...])

time: 120 us -> 114 us (0.950)
  Pallas kernels: 114 us -> 107 us
    pallas_call x1, Pallas kernels: 114 us -> 107 us  [on_device(): pl.pallas_call(kernel, out_shape=(jax.ShapeDtypeStruct((NODES, WIDTH), BF...]
where the time goes in v4:
time: 114 us
  Pallas kernels  107 us (94%)
  local copies, waits for them, and re-layouts  2.98 us (3%)
  other arithmetic  2.89 us (3%)
    pallas_call x1, Pallas kernels, on_device(): pl.pallas_call(kernel, out_shape=(jax.ShapeDtypeStruct((NODES, WIDTH), BF...  107 us
    unnamed x7, local copies, waits for them, and re-layouts  2.98 us
    convert_element_type x1, other arithmetic, on_device(): return (embeddings, embed_grad, clicks, mean.astype(F32))  2.89 us

profile of v4, /device:TPU:1, one launch (start us, length us, event | category | flops | bytes accessed | tf_op | source)
XLA Modules:
  0.0 113.9 jit_solution(6205259731742499734)
XLA Ops:
  0.6 107.4 %shard_map.138 = (bf16[256,512]{1,0:T(8,128)(2,1)}, f32[256,512]{1,0:T(8,128)}, f32[8]{0:T(128)}, bf16[1024,512]{1,0:T(8,128)(2,1)}) custom-call(bf16[256,512]{1,0:T(8,128)(2,1)} %feats.1, s32[1,16,32]{2,1,0:T(8,128)} %send_rows.1, s32[16,256]{1,0:T(8,128)} %bitcast.3, f32[16,256]{1,0:T(8,128)} %bitcast.4, bf16[1024,512]{1,0:T(8,128)(2,1)} %gcn_hbm.1, ...), custom_call_target="tpu_custom_call" | custom-call | tf_op jit(solution)/shard_map/pallas_call | solution.py:707
  108.0 0.0 copy-start
  108.0 0.0 copy-start.1
  108.0 2.9 %convert_element_type.3 = f32[1024,512]{1,0:T(8,128)} convert(bf16[1024,512]{1,0:T(8,128)(2,1)} %get-tuple-element.11) | non-fusion elementwise | flops 524288 | bytes 3145728 | tf_op jit(solution)/shard_map/convert_element_type | solution.py:790
  110.9 1.7 %copy.18 = bf16[256,512]{1,0:T(8,128)(2,1)} copy(bf16[256,512]{1,0:T(8,128)(2,1)} %get-tuple-element.16) | data formatting | bytes 524288
  112.6 0.0 copy-done
  112.6 0.8 copy.19
  113.4 0.0 copy-done.1
  113.4 0.5 copy.20
Async XLA Ops:
  108.0 4.6 %copy-start = (f32[256,512]{1,0:T(8,128)S(1)}, f32[256,512]{1,0:T(8,128)}, u32[]{:S(2)}) copy-start(f32[256,512]{1,0:T(8,128)} %get-tuple-element.17) | copy-start | bytes 1572868
  108.0 5.4 %copy-start.1 = (f32[8]{0:T(128)S(1)}, f32[8]{0:T(128)}, u32[]{:S(2)}) copy-start(f32[8]{0:T(128)} %get-tuple-element.18) | copy-start | bytes 100
